TPU v7x, 32 devices: a whole 2x2x4 slice. The times are simulated.
32 devices in a mesh: rep: 2 (over y), section: 2 (over core), seq: 8 (over z, x).
Axes of the slice: x: 2, y: 2, z: 4, core: 2. Of those that a mesh axis runs over, the one named last changes fastest.
Arguments:
- qkv_all: bfloat16 [2, 2, 128, 12288], P(None, 'section', ('rep', 'seq')), parts along dimension 2, may hold values from -120 to 120
- context_kv: bfloat16 [128, 8192], P(('rep', 'section', 'seq')), parts along dimension 0, may hold values from -6 to 6
Outputs:
- attended: bfloat16 [2, 2, 128, 4096], P(None, 'section', ('rep', 'seq')), parts along dimension 2
There are 2 independent parts, one for each index of `rep`. A program takes and returns all parts, laid end to end along the dimension named above; each array names one. Nothing has to cross between parts.
All inputs are finite; a program needn't handle non-finite values.
Results may differ from a plain program's by a relative error of at most 0.005.
Values may be sent and summed in bfloat16 or wider, within the bound.
No kernel may reach another device: no remote copies, remote signals or barrier semaphores. Data moves between devices by JAX's collectives and lax.ppermute only.
A program may use at most 64 MiB of HBM per device.

v0:
```python
import jax
import jax.numpy as jnp
from jax import lax
from jax.sharding import PartitionSpec as P

HEADS = 32


def from_root(value, axis, source):
    kept = jnp.where(lax.axis_index(axis) == source, value, 0).astype(value.dtype)
    return lax.psum(kept, axis)


def block_length(key_count):
    if key_count % 256 == 0:
        return 256
    return key_count


def attend(queries, key_sets, score_scale):
    query_count = queries.shape[0]
    local_heads = queries.shape[1]
    head_dim = queries.shape[2]
    run_max = jnp.full((local_heads, query_count), -jnp.inf, jnp.float32)
    run_sum = jnp.zeros((local_heads, query_count), jnp.float32)
    run_acc = jnp.zeros((local_heads, query_count, head_dim), jnp.float32)
    for key_set in key_sets:
        block_len = block_length(key_set.shape[0])
        key_blocks = key_set.reshape(
            key_set.shape[0] // block_len, block_len, local_heads, 2 * head_dim
        )

        def one_block(running, block):
            old_max, old_sum, old_acc = running
            block_keys = block[:, :, :head_dim]
            block_vals = block[:, :, head_dim:]
            scores = (
                jnp.einsum("qhd,khd->hqk", queries, block_keys, preferred_element_type=jnp.float32)
                * score_scale
            )
            new_max = jnp.maximum(old_max, jnp.max(scores, axis=2))
            rescale = jnp.exp(old_max - new_max)
            weights = jnp.exp(scores - new_max[:, :, None])
            new_sum = old_sum * rescale + jnp.sum(weights, axis=2)
            new_acc = old_acc * rescale[:, :, None] + jnp.einsum(
                "hqk,khd->hqd",
                weights.astype(jnp.bfloat16),
                block_vals,
                preferred_element_type=jnp.float32,
            )
            return ((new_max, new_sum, new_acc), None)

        (run_max, run_sum, run_acc), _ = lax.scan(
            one_block, (run_max, run_sum, run_acc), key_blocks
        )
    return (run_max, run_sum, run_acc)


def spread_rows(source, groups, copies):
    row_count = source.shape[0]
    lane_count = source.shape[2]
    split_view = source.reshape(copies, row_count // copies, groups, lane_count)
    return split_view.transpose(2, 0, 1, 3).reshape(
        groups * copies, row_count // copies, lane_count
    )


def repeat_rows(source, groups, copies):
    row_count = source.shape[0]
    lane_count = source.shape[2]
    group_first = source.transpose(1, 0, 2)[:, None]
    return jnp.broadcast_to(group_first, (groups, copies, row_count, lane_count)).reshape(
        groups * copies, row_count, lane_count
    )


def shards(qkv_all, context_kv):
    seq_count = lax.axis_size("seq")
    groups = min(seq_count, HEADS)
    copies = seq_count // groups
    per_group = HEADS // groups
    steps = qkv_all.shape[0]
    tok_rows = qkv_all.shape[2]
    head_dim = qkv_all.shape[3] // (3 * HEADS)
    group_width = per_group * head_dim
    score_scale = head_dim ** (-0.5)
    context_rows = context_kv.reshape(context_kv.shape[0], groups, 2 * group_width)
    context_local = lax.all_to_all(
        repeat_rows(context_rows, groups, copies), "seq", split_axis=0, concat_axis=0, tiled=True
    )
    context_all = lax.all_gather(context_local, "section", axis=0, tiled=True)
    key_sets = [context_all.reshape(-1, per_group, 2 * head_dim)]
    results = []
    for step in range(steps):
        frames = qkv_all[step, 0].reshape(tok_rows, groups, per_group, 3, head_dim)
        queries = frames[:, :, :, 0].reshape(tok_rows, groups, group_width)
        key_vals = frames[:, :, :, 1:].reshape(tok_rows, groups, 2 * group_width)
        query_got, key_got = (
            lax.all_to_all(
                spread_rows(queries, groups, copies), "seq", split_axis=0, concat_axis=0, tiled=True
            ),
            lax.all_to_all(
                repeat_rows(key_vals, groups, copies),
                "seq",
                split_axis=0,
                concat_axis=0,
                tiled=True,
            ),
        )
        own_keys = key_got.reshape(-1, per_group, 2 * head_dim)
        query_rows = query_got.reshape(-1, per_group, head_dim)
        run_max, run_sum, run_acc = attend(query_rows, key_sets + [own_keys], score_scale)
        finished = (run_acc / run_sum[:, :, None]).astype(jnp.bfloat16)
        finished = finished.transpose(1, 0, 2).reshape(seq_count, tok_rows // copies, group_width)
        returned = lax.all_to_all(finished, "seq", split_axis=0, concat_axis=0, tiled=True)
        merged = (
            returned.reshape(groups, copies, tok_rows // copies, group_width)
            .transpose(1, 2, 0, 3)
            .reshape(tok_rows, HEADS * head_dim)
        )
        results.append(merged)
        if step + 1 < steps:
            cleanest = from_root(own_keys, "section", lax.axis_size("section") - 1)
            key_sets = key_sets + [cleanest]
    return jnp.stack(results)[:, None]


def solution(mesh):
    in_specs = (P(None, "section", ("rep", "seq"), None), P(("rep", "section", "seq"), None))
    out_specs = P(None, "section", ("rep", "seq"), None)
    return jax.shard_map(shards, mesh=mesh, in_specs=in_specs, out_specs=out_specs, check_vma=False)
```

profile of v0, /device:TPU:0, one launch (start us, length us, event | category | flops | bytes accessed | tf_op | source)
XLA Modules:
  0.0 101.8 jit_solution(7023640201374418829)
XLA Ops:
  6.5 7.3 %all-to-all-start.1 = ((bf16[8,4,1024]{2,1,0:T(4,128)(2,1)}), bf16[8,4,1024]{2,1,0:T(4,128)(2,1)S(1)}, u32[]{:S(2)}, u32[]{:S(2)}) async-start(bf16[8,4,1024]{2,1,0:T(4,128)(2,1)} %bitcast.133), calls=%async_computation.1 | async-start | bytes 131072 | tf_op jit(solution)/shard_map/all_to_all | solution.py:88
  13.8 1.0 %fusion.62 = (bf16[1,1,8,12288]{3,2,1,0:T(8,128)(2,1)S(1)}, bf16[1,1,8,12288]{3,2,1,0:T(8,128)(2,1)S(1)}) fusion(bf16[2,1,8,12288]{3,2,1,0:T(8,128)(2,1)} %param.2), kind=kLoop, calls=%fused_computation.84 | loop fusion | bytes 786432 | tf_op jit(solution)/shard_map/slice | solution.py:95
  14.8 0.3 reshape_squeeze.6
  15.1 0.4 slice_reduce_fusion.1
  15.5 0.1 slice.71
  15.7 0.1 reshape.120
  15.7 0.7 copy.61
  16.5 0.6 copy.56
  17.1 0.3 reshape_squeeze.7
  17.4 0.1 slice.77
  17.6 0.1 reshape.125
  17.6 0.7 copy.73
  18.4 0.4 slice_reduce_fusion
  18.8 0.6 copy.67
  19.4 1.3 %all-to-all-done.1 = bf16[8,4,1024]{2,1,0:T(4,128)(2,1)S(1)} async-done(((bf16[8,4,1024]{2,1,0:T(4,128)(2,1)}), bf16[8,4,1024]{2,1,0:T(4,128)(2,1)S(1)}, u32[]{:S(2)}, u32[]{:S(2)}) %all-to-all-start.1) | async-done | bytes 65568 | tf_op jit(solution)/shard_map/all_to_all | solution.py:88
  20.7 4.7 %all-to-all-start.4 = ((bf16[8,8,512]{2,1,0:T(8,128)(2,1)}), bf16[8,8,512]{2,1,0:T(8,128)(2,1)S(1)}, u32[]{:S(2)}, u32[]{:S(2)}) async-start(bf16[8,8,512]{2,1,0:T(8,128)(2,1)} %copy.67), calls=%async_computation.4 | async-start | bytes 131072 | tf_op jit(solution)/shard_map/all_to_all | solution.py:99
  25.4 1.9 %all_gather.3 = bf16[16,4,1024]{2,1,0:T(4,128)(2,1)S(1)} all-gather(bf16[8,4,1024]{2,1,0:T(4,128)(2,1)S(1)} %all-to-all-done.1), channel_id=1, replica_groups=mesh['rep'=2,'section'=2,'seq'=8] {'section'}, dimensions={0}, use_global_device_ids=true | all-gather | bytes 196608 | tf_op jit(solution)/shard_map/all_gather | solution.py:91
  27.3 0.1 squeeze.17
  27.4 4.9 %all-to-all-done.4 = bf16[8,8,512]{2,1,0:T(8,128)(2,1)S(1)} async-done(((bf16[8,8,512]{2,1,0:T(8,128)(2,1)}), bf16[8,8,512]{2,1,0:T(8,128)(2,1)S(1)}, u32[]{:S(2)}, u32[]{:S(2)}) %all-to-all-start.4) | async-done | bytes 65568 | tf_op jit(solution)/shard_map/all_to_all | solution.py:99
  32.3 3.3 %all-to-all-start = ((bf16[8,8,512]{2,1,0:T(8,128)(2,1)}), bf16[8,8,512]{2,1,0:T(8,128)(2,1)S(1)}, u32[]{:S(2)}, u32[]{:S(2)}) async-start(bf16[8,8,512]{2,1,0:T(8,128)(2,1)} %copy.56), calls=%async_computation | async-start | bytes 131072 | tf_op jit(solution)/shard_map/all_to_all | solution.py:99
  35.7 0.2 fusion.67
  35.9 6.6 %all-to-all-done = bf16[8,8,512]{2,1,0:T(8,128)(2,1)S(1)} async-done(((bf16[8,8,512]{2,1,0:T(8,128)(2,1)}), bf16[8,8,512]{2,1,0:T(8,128)(2,1)S(1)}, u32[]{:S(2)}, u32[]{:S(2)}) %all-to-all-start) | async-done | bytes 65568 | tf_op jit(solution)/shard_map/all_to_all | solution.py:99
  42.5 3.4 %all-to-all-start.2 = ((bf16[8,8,1024]{2,1,0:T(8,128)(2,1)}), bf16[8,8,1024]{2,1,0:T(8,128)(2,1)S(1)}, u32[]{:S(2)}, u32[]{:S(2)}) async-start(bf16[8,8,1024]{2,1,0:T(8,128)(2,1)} %copy.61), calls=%async_computation.2 | async-start | bytes 262144 | tf_op jit(solution)/shard_map/all_to_all | solution.py:102
  45.9 0.2 fusion.69
  46.1 7.1 %all-to-all-done.2 = bf16[8,8,1024]{2,1,0:T(8,128)(2,1)S(1)} async-done(((bf16[8,8,1024]{2,1,0:T(8,128)(2,1)}), bf16[8,8,1024]{2,1,0:T(8,128)(2,1)S(1)}, u32[]{:S(2)}, u32[]{:S(2)}) %all-to-all-start.2) | async-done | bytes 131104 | tf_op jit(solution)/shard_map/all_to_all | solution.py:102
  53.2 3.4 %all-to-all-start.5 = ((bf16[8,8,1024]{2,1,0:T(8,128)(2,1)}), bf16[8,8,1024]{2,1,0:T(8,128)(2,1)S(1)}, u32[]{:S(2)}, u32[]{:S(2)}) async-start(bf16[8,8,1024]{2,1,0:T(8,128)(2,1)} %copy.73), calls=%async_computation.5 | async-start | bytes 262144 | tf_op jit(solution)/shard_map/all_to_all | solution.py:102
  56.6 0.1 squeeze.18
  56.7 0.7 fusion.63
  57.4 0.2 fusion.70
  57.6 0.1 fusion.13
  57.7 0.2 fusion.6
  57.9 0.2 fusion.12
  58.1 0.1 copy.66
  58.2 0.6 reshape.121
  58.8 5.0 %all-to-all-done.5 = bf16[8,8,1024]{2,1,0:T(8,128)(2,1)S(1)} async-done(((bf16[8,8,1024]{2,1,0:T(8,128)(2,1)}), bf16[8,8,1024]{2,1,0:T(8,128)(2,1)S(1)}, u32[]{:S(2)}, u32[]{:S(2)}) %all-to-all-start.5) | async-done | bytes 131104 | tf_op jit(solution)/shard_map/all_to_all | solution.py:102
  63.8 3.3 %all-to-all-start.3 = ((bf16[8,8,512]{2,1,0:T(8,128)(2,1)}), bf16[8,8,512]{2,1,0:T(8,128)(2,1)S(1)}, u32[]{:S(2)}, u32[]{:S(2)}) async-start(bf16[8,8,512]{2,1,0:T(8,128)(2,1)} %reshape.121), calls=%async_computation.3 | async-start | bytes 131072 | tf_op jit(solution)/shard_map/all_to_all | solution.py:115
  67.2 0.1 squeeze.19
  67.3 0.2 fusion.66
  67.5 11.5 %all-reduce.2.cloned.1.call-done = bf16[64,4,256]{2,0,1:T(8,128)(2,1)} async-done(((bf16[64,4,256]{2,0,1:T(8,128)(2,1)}), bf16[64,4,256]{2,0,1:T(8,128)(2,1)}) %all-reduce.2.cloned.1.call-update) | async-done | bytes 131088 | tf_op jit(solution)/shard_map/psum | solution.py:11
  79.0 1.1 %fusion.68 = (f32[4,64]{1,0:T(4,128)S(1)}, f32[4,64,64]{2,1,0:T(8,128)S(1)}) fusion(bf16[64,4,128]{2,1,0:T(4,128)(2,1)S(1)} %reshape.124, bf16[64,4,256]{2,0,1:T(8,128)(2,1)} %all-reduce.2.cloned.1.call-done), kind=kOutput, calls=%fused_computation.90 | convolution fusion | flops 4226816 | bytes 197632 | tf_op jit(solution)/shard_map/while/body/eval_jaxpr/qhd,khd->hqk/dot_general | solution.py:38
  80.2 0.2 fusion.19
  80.4 0.2 fusion.8
  80.6 0.7 copy-done
  81.3 0.2 fusion.9
  81.5 0.2 fusion.11
  81.7 0.1 copy.78
  81.9 12.5 %all_to_all.35 = bf16[8,8,512]{2,1,0:T(8,128)(2,1)S(1)} all-to-all(bf16[8,8,512]{2,1,0:T(8,128)(2,1)S(1)} %reshape.126), channel_id=1, replica_groups=mesh['rep'=2,'section'=2,'seq'=8] {'seq'}, dimensions={0} | all-to-all | bytes 131072 | tf_op jit(solution)/shard_map/all_to_all | solution.py:115
  94.3 0.7 maximum_bitcast_fusion
  (17 shorter events, 0.4 us)
Async XLA Ops:
  6.5 14.2 %all-to-all-start.1 = ((bf16[8,4,1024]{2,1,0:T(4,128)(2,1)}), bf16[8,4,1024]{2,1,0:T(4,128)(2,1)S(1)}, u32[]{:S(2)}, u32[]{:S(2)}) async-start(bf16[8,4,1024]{2,1,0:T(4,128)(2,1)} %bitcast.133), calls=%async_computation.1 | async-start | bytes 131072 | tf_op jit(solution)/shard_map/all_to_all | solution.py:88
  20.7 11.6 %all-to-all-start.4 = ((bf16[8,8,512]{2,1,0:T(8,128)(2,1)}), bf16[8,8,512]{2,1,0:T(8,128)(2,1)S(1)}, u32[]{:S(2)}, u32[]{:S(2)}) async-start(bf16[8,8,512]{2,1,0:T(8,128)(2,1)} %copy.67), calls=%async_computation.4 | async-start | bytes 131072 | tf_op jit(solution)/shard_map/all_to_all | solution.py:99
  32.3 10.2 %all-to-all-start = ((bf16[8,8,512]{2,1,0:T(8,128)(2,1)}), bf16[8,8,512]{2,1,0:T(8,128)(2,1)S(1)}, u32[]{:S(2)}, u32[]{:S(2)}) async-start(bf16[8,8,512]{2,1,0:T(8,128)(2,1)} %copy.56), calls=%async_computation | async-start | bytes 131072 | tf_op jit(solution)/shard_map/all_to_all | solution.py:99
  42.5 10.7 %all-to-all-start.2 = ((bf16[8,8,1024]{2,1,0:T(8,128)(2,1)}), bf16[8,8,1024]{2,1,0:T(8,128)(2,1)S(1)}, u32[]{:S(2)}, u32[]{:S(2)}) async-start(bf16[8,8,1024]{2,1,0:T(8,128)(2,1)} %copy.61), calls=%async_computation.2 | async-start | bytes 262144 | tf_op jit(solution)/shard_map/all_to_all | solution.py:102
  53.2 10.7 %all-to-all-start.5 = ((bf16[8,8,1024]{2,1,0:T(8,128)(2,1)}), bf16[8,8,1024]{2,1,0:T(8,128)(2,1)S(1)}, u32[]{:S(2)}, u32[]{:S(2)}) async-start(bf16[8,8,1024]{2,1,0:T(8,128)(2,1)} %copy.73), calls=%async_computation.5 | async-start | bytes 262144 | tf_op jit(solution)/shard_map/all_to_all | solution.py:102
  56.6 22.4 %all-reduce.2.cloned.1.call-start = ((), (), s32[]{:S(2)}) async-start(), calls=%async_computation.7 | async-start | bytes 262144 | tf_op jit(solution)/shard_map/psum | solution.py:11
  63.8 18.0 %all-to-all-start.3 = ((bf16[8,8,512]{2,1,0:T(8,128)(2,1)}), bf16[8,8,512]{2,1,0:T(8,128)(2,1)S(1)}, u32[]{:S(2)}, u32[]{:S(2)}) async-start(bf16[8,8,512]{2,1,0:T(8,128)(2,1)} %reshape.121), calls=%async_computation.3 | async-start | bytes 131072 | tf_op jit(solution)/shard_map/all_to_all | solution.py:115
  80.4 0.9 copy-start
Sparse Core Ops, SparseCore 0:
  59.7 19.2 all-reduce.1
where the time goes:
time: 103 us; the launch traced here: 102 us
  waiting for transfers between devices  36.4 us (35%)
  starting transfers between devices  25.5 us (25%)
  blocking collectives  14.4 us (14%)
  between operations  13.6 us (13%)
  local copies, waits for them, and re-layouts  7.37 us (7%)
  matrix products  2.92 us (3%)
  other arithmetic  1.74 us (2%)
    all_to_all x1, blocking collectives, shards(): lax.all_to_all(finished, 'seq', split_axis=0, concat_axis=0, tiled=True)  12.5 us
    all_to_all x2, waiting for transfers between devices, shards(): lax.all_to_all(repeat_rows(key_vals, groups, copies), 'seq', split_axis=0...  12.1 us
    psum x1, waiting for transfers between devices, from_root(): return lax.psum(kept, axis)  11.5 us
    all_to_all x2, waiting for transfers between devices, shards(): lax.all_to_all(spread_rows(queries, groups, copies), 'seq', split_axis=0,...  11.5 us
    all_to_all x2, starting transfers between devices, shards(): lax.all_to_all(spread_rows(queries, groups, copies), 'seq', split_axis=0,...  8.08 us
    all_to_all x1, starting transfers between devices, shards(): lax.all_to_all(repeat_rows(context_rows, groups, copies), 'seq', split_ax...  7.25 us
    all_to_all x2, starting transfers between devices, shards(): lax.all_to_all(repeat_rows(key_vals, groups, copies), 'seq', split_axis=0...  6.74 us
    all_to_all x1, starting transfers between devices, shards(): lax.all_to_all(finished, 'seq', split_axis=0, concat_axis=0, tiled=True)  3.35 us
  transfers between devices with their start and end apart: 7, of which 6 were waited for; matrix products, arithmetic and copies ran while one was open for 11% of the time, Pallas kernels for 0%

commit v1 on v0

v1 whole, which is shorter than its diff:
```python
import functools

import jax
import jax.numpy as jnp
from jax import lax
from jax.experimental import pallas as pl
from jax.experimental.pallas import tpu as pltpu
from jax.sharding import PartitionSpec as P

HEADS = 32
AXES = ("section", "seq")


def softmax_mix(queries, keys, values, scale):
    scores = (
        lax.dot_general(
            queries, keys, (((1,), (1,)), ((), ())), preferred_element_type=jnp.float32
        )
        * scale
    )
    weights = jnp.exp(scores - jnp.max(scores, axis=1, keepdims=True))
    total = jnp.sum(weights, axis=1, keepdims=True)
    mixed = jnp.dot(weights.astype(jnp.bfloat16), values, preferred_element_type=jnp.float32)
    return (mixed / total).astype(jnp.bfloat16)


def attend_kernel(
    steps, sections, heads, tok_rows, ctx_rows, head_dim, scale, got_ref, out_ref
):
    sources = got_ref.shape[0]
    per_section = sources // sections
    ctx_base = steps * heads * 3 * tok_rows

    def part(step, section, head, role):
        base = ((step * heads + head) * 3 + role) * tok_rows
        block = got_ref[section * per_section : (section + 1) * per_section, base : base + tok_rows]
        return block.reshape(per_section * tok_rows, head_dim)

    ctx_all = got_ref[:, ctx_base:]

    def context(head, role):
        base = (head * 2 + role) * ctx_rows
        return ctx_all[:, base : base + ctx_rows].reshape(sources * ctx_rows, head_dim)

    for head in range(heads):
        earlier_keys = [context(head, 0)]
        earlier_vals = [context(head, 1)]
        for step in range(steps):
            own = [(part(step, s, head, 1), part(step, s, head, 2)) for s in range(sections)]
            for s in range(sections):
                keys = jnp.concatenate(earlier_keys + [own[s][0]], axis=0)
                vals = jnp.concatenate(earlier_vals + [own[s][1]], axis=0)
                mixed = softmax_mix(part(step, s, head, 0), keys, vals, scale)
                base = (step * heads + head) * tok_rows
                out_ref[s * per_section : (s + 1) * per_section, base : base + tok_rows] = (
                    mixed.reshape(per_section, tok_rows, head_dim)
                )
            earlier_keys.append(own[sections - 1][0])
            earlier_vals.append(own[sections - 1][1])


def shards(qkv_all, context_kv):
    sections = lax.axis_size("section")
    peers = sections * lax.axis_size("seq")
    groups = min(peers, HEADS)
    copies = peers // groups
    heads = HEADS // groups
    steps, _, tok_rows, width = qkv_all.shape
    head_dim = width // (3 * HEADS)
    ctx_rows = context_kv.shape[0]
    scale = head_dim ** (-0.5)
    if copies > 1:
        return shards_copied(qkv_all, context_kv, sections, groups, copies, heads, scale)

    blocks = qkv_all[:, 0].reshape(steps, tok_rows, groups, heads * 3, head_dim)
    blocks = blocks.transpose(2, 0, 3, 1, 4).reshape(groups, -1, head_dim)
    ctx = context_kv.reshape(ctx_rows, groups, heads * 2, head_dim)
    ctx = ctx.transpose(1, 2, 0, 3).reshape(groups, -1, head_dim)
    sent = jnp.concatenate([blocks, ctx], axis=1)
    got = lax.all_to_all(sent, AXES, split_axis=0, concat_axis=0, tiled=True)
    mixed = pl.pallas_call(
        functools.partial(
            attend_kernel, steps, sections, heads, tok_rows, ctx_rows, head_dim, scale
        ),
        out_shape=jax.ShapeDtypeStruct((peers, steps * heads * tok_rows, head_dim), jnp.bfloat16),
        in_specs=[pl.BlockSpec(memory_space=pltpu.VMEM)],
        out_specs=pl.BlockSpec(memory_space=pltpu.VMEM),
        compiler_params=pltpu.CompilerParams(vmem_limit_bytes=32 * 1024 * 1024),
    )(got)
    back = lax.all_to_all(mixed, AXES, split_axis=0, concat_axis=0, tiled=True)
    back = back.reshape(groups, steps, heads, tok_rows, head_dim).transpose(1, 3, 0, 2, 4)
    return back.reshape(steps, 1, tok_rows, HEADS * head_dim)


def shards_copied(qkv_all, context_kv, sections, groups, copies, heads, scale):
    steps, _, tok_rows, width = qkv_all.shape
    head_dim = width // (3 * HEADS)
    peers = groups * copies
    share = tok_rows // copies
    ctx_rows = context_kv.shape[0]
    frames = qkv_all[:, 0].reshape(steps, tok_rows, groups, heads, 3, head_dim)
    queries = frames[..., 0, :].reshape(steps, copies, share, groups, heads, head_dim)
    queries = queries.transpose(3, 1, 0, 4, 2, 5).reshape(peers, -1, head_dim)
    key_vals = frames[..., 1:, :].transpose(2, 0, 3, 4, 1, 5).reshape(groups, -1, head_dim)
    ctx = context_kv.reshape(ctx_rows, groups, heads, 2, head_dim)
    ctx = ctx.transpose(1, 2, 3, 0, 4).reshape(groups, -1, head_dim)
    shared = jnp.concatenate([key_vals, ctx], axis=1)
    shared = jnp.broadcast_to(shared[:, None], (groups, copies) + shared.shape[1:])
    shared = shared.reshape((peers,) + shared.shape[2:])
    sent = jnp.concatenate([queries, shared], axis=1)
    got = lax.all_to_all(sent, AXES, split_axis=0, concat_axis=0, tiled=True)
    per_section = peers // sections
    cut = steps * heads * share
    end = cut + steps * heads * 2 * tok_rows
    q = got[:, :cut].reshape(sections, per_section, steps, heads, share, head_dim)
    q = q.transpose(2, 0, 3, 1, 4, 5).reshape(steps, sections, heads, -1, head_dim)
    kv = got[:, cut:end].reshape(sections, per_section, steps, heads, 2, tok_rows, head_dim)
    kv = kv.transpose(2, 0, 4, 3, 1, 5, 6).reshape(steps, sections, 2, heads, -1, head_dim)
    ctx = got[:, end:].reshape(peers, heads, 2, ctx_rows, head_dim)
    earlier = [ctx.transpose(2, 1, 0, 3, 4).reshape(2, heads, -1, head_dim)]
    results = []
    for step in range(steps):
        for s in range(sections):
            keys, vals = jnp.concatenate(earlier + [kv[step, s]], axis=2)
            results.append(
                jnp.stack([softmax_mix(q[step, s, h], keys[h], vals[h], scale) for h in range(heads)])
            )
        earlier = earlier + [kv[step, sections - 1]]
    mixed = jnp.stack(results).reshape(steps, sections, heads, per_section, share, head_dim)
    mixed = mixed.transpose(1, 3, 0, 2, 4, 5).reshape(peers, -1, head_dim)
    back = lax.all_to_all(mixed, AXES, split_axis=0, concat_axis=0, tiled=True)
    back = back.reshape(groups, copies, steps, heads, share, head_dim)
    back = back.transpose(2, 1, 4, 0, 3, 5)
    return back.reshape(steps, 1, tok_rows, HEADS * head_dim)


def solution(mesh):
    in_specs = (P(None, "section", ("rep", "seq"), None), P(("rep", "section", "seq"), None))
    out_specs = P(None, "section", ("rep", "seq"), None)
    return jax.shard_map(shards, mesh=mesh, in_specs=in_specs, out_specs=out_specs, check_vma=False)
```

time: 103 us -> 35.9 us (0.35)
  waiting for transfers between devices: 36.4 us -> 0 us
  starting transfers between devices: 25.5 us -> 0 us
  blocking collectives: 14.4 us -> 31.8 us
  between operations: 13.6 us -> 0.03 us
  local copies, waits for them, and re-layouts: 7.37 us -> 1.72 us
  matrix products: 2.92 us -> 0 us
  Pallas kernels: 0 us -> 2.08 us
  other arithmetic: 1.74 us -> 0.03 us
    all_to_all x6 -> x0, starting transfers between devices: 25.4 us -> none  [the longest x2 8.08 us: shards(): lax.all_to_all(spread_rows(queries, groups, copies), 'seq', split_axis=0,...]
    all_to_all x6 -> x0, waiting for transfers between devices: 24.9 us -> none  [the longest x2 12.1 us: shards(): lax.all_to_all(repeat_rows(key_vals, groups, copies), 'seq', split_axis=0...]
    all_to_all x1 -> x2, blocking collectives: 12.5 us -> 31.8 us  [the longest x1 21.6 us: shards(): got = lax.all_to_all(sent, AXES, split_axis=0, concat_axis=0, tiled=True)]
    psum x1 -> x0, waiting for transfers between devices: 11.5 us -> none  [from_root(): return lax.psum(kept, axis)]
    dot_general x10 -> x0, matrix products: 2.92 us -> none  [the longest x5 1.79 us: one_block(): jnp.einsum('qhd,khd->hqk', queries, block_keys, preferred_element_type=jn...]
    reshape x8 -> x0, local copies, waits for them, and re-layouts: 2.15 us -> none  [the longest x2 1.29 us: spread_rows(): split_view.transpose(2, 0, 1, 3)]
    slice x7 -> x0, local copies, waits for them, and re-layouts: 2.15 us -> none  [the longest x1 1.05 us: shards(): frames = qkv_all[step, 0].reshape(tok_rows, groups, per_group, 3, head_dim)]
    pallas_call x0 -> x1, Pallas kernels: none -> 2.08 us  [shards(): pl.pallas_call(functools.partial(attend_kernel, steps, sections, heads, t...]
  transfers between devices with their start and end apart: 7 -> 0, of which waited for: 6 -> 0; matrix products, arithmetic and copies ran while one was open for 11% -> 0% of each run, Pallas kernels for 0% -> 0%
where the time goes in v1:
time: 35.9 us; the launch traced here: 35.7 us
  blocking collectives  31.8 us (89%)
  Pallas kernels  2.08 us (6%)
  local copies, waits for them, and re-layouts  1.72 us (5%)
    all_to_all x1, blocking collectives, shards(): got = lax.all_to_all(sent, AXES, split_axis=0, concat_axis=0, tiled=True)  21.6 us
    all_to_all x1, blocking collectives, shards(): back = lax.all_to_all(mixed, AXES, split_axis=0, concat_axis=0, tiled=True)  10.2 us
    pallas_call x1, Pallas kernels, shards(): pl.pallas_call(functools.partial(attend_kernel, steps, sections, heads, t...  2.08 us
    another operation x1, local copies, waits for them, and re-layouts, shards(): blocks = qkv_all[:, 0].reshape(steps, tok_rows, groups, heads * 3, head_dim)  1.05 us

profile of v1, /device:TPU:0, one launch (start us, length us, event | category | flops | bytes accessed | tf_op | source)
XLA Modules:
  0.0 35.7 jit_solution(11259336932817841219)
XLA Ops:
  0.0 0.0 copy-start
  0.0 1.1 %copy.3 = bf16[2,8,16,6,128]{4,1,3,0,2:T(8,128)(2,1)S(1)} copy(bf16[2,8,16,6,128]{4,1,3,2,0:T(8,128)(2,1)} %bitcast.15) | data formatting | bytes 786432 | tf_op jit(solution)/shard_map/reshape;squeeze | solution.py:75
  1.1 0.0 copy-done
  1.1 21.6 %all_to_all.10.got_ref = bf16[16,112,128]{2,1,0:T(8,128)(2,1)S(1)} all-to-all(bf16[16,112,128]{2,1,0:T(8,128)(2,1)S(1)} %pad_maximum_fusion), channel_id=1, replica_groups=mesh['rep'=2,'section'=2,'seq'=8] {'section','seq'}, dimensions={0} | all-to-all | bytes 917504 | tf_op jit(solution)/shard_map/all_to_all | solution.py:80
  22.7 2.1 %shard_map.28 = bf16[16,32,128]{2,1,0:T(8,128)(2,1)S(1)} custom-call(bf16[16,112,128]{2,1,0:T(8,128)(2,1)S(1)} %all_to_all.10.got_ref), custom_call_target="tpu_custom_call" | custom-call | tf_op jit(solution)/shard_map/pallas_call | solution.py:81
  24.8 10.2 %all_to_all.11 = bf16[16,32,128]{2,1,0:T(8,128)(2,1)S(1)} all-to-all(bf16[16,32,128]{2,1,0:T(8,128)(2,1)S(1)} %shard_map.28), channel_id=1, replica_groups=mesh['rep'=2,'section'=2,'seq'=8] {'section','seq'}, dimensions={0} | all-to-all | bytes 262144 | tf_op jit(solution)/shard_map/all_to_all | solution.py:90
  35.0 0.7 %copy.5 = bf16[2,8,16,2,128]{4,1,3,2,0:T(8,128)(2,1)} copy(bf16[2,8,16,2,128]{4,1,3,0,2:T(8,128)(2,1)S(1)} %bitcast.14) | data formatting | bytes 262144 | tf_op jit(solution)/shard_map/transpose | solution.py:91
  (1 shorter events, 0.0 us)
Async XLA Ops:
  0.0 1.1 %copy-start = (bf16[4,8192]{1,0:T(4,128)(2,1)S(1)}, bf16[4,8192]{1,0:T(4,128)(2,1)}, u32[]{:S(2)}) copy-start(bf16[4,8192]{1,0:T(4,128)(2,1)} %param.3) | copy-start | bytes 196612

commit v2 on v1

--- a/solution.py
+++ b/solution.py
@@ -25,8 +25,9 @@
 
 
 def attend_kernel(
-    steps, sections, heads, tok_rows, ctx_rows, head_dim, scale, got_ref, out_ref
+    steps, sections, heads, tok_rows, ctx_rows, head_dim, scale, got_ref, *refs
 ):
+    out_refs, out_ref = refs[:-1], refs[-1]
     sources = got_ref.shape[0]
     per_section = sources // sections
     ctx_base = steps * heads * 3 * tok_rows
@@ -57,6 +58,22 @@
                 )
             earlier_keys.append(own[sections - 1][0])
             earlier_vals.append(own[sections - 1][1])
+    me = lax.axis_index("section") * per_section + lax.axis_index("seq")
+    for offset, piece_ref in enumerate(out_refs):
+        piece_ref[...] = out_ref[lax.rem(me + offset, sources)]
+
+
+def place_kernel(steps, sections, heads, tok_rows, head_dim, *refs):
+    piece_refs, out_ref = refs[:-1], refs[-1]
+    sources = len(piece_refs)
+    me = lax.axis_index("section") * (sources // sections) + lax.axis_index("seq")
+    for offset, piece_ref in enumerate(piece_refs):
+        owner = lax.rem(me + sources - offset, sources)
+        for step in range(steps):
+            for head in range(heads):
+                base = (step * heads + head) * tok_rows
+                column = pl.multiple_of((owner * heads + head) * head_dim, head_dim)
+                out_ref[step, 0, :, pl.ds(column, head_dim)] = piece_ref[base : base + tok_rows]
 
 
 def shards(qkv_all, context_kv):
@@ -78,18 +95,30 @@
     ctx = ctx.transpose(1, 2, 0, 3).reshape(groups, -1, head_dim)
     sent = jnp.concatenate([blocks, ctx], axis=1)
     got = lax.all_to_all(sent, AXES, split_axis=0, concat_axis=0, tiled=True)
-    mixed = pl.pallas_call(
+    piece = jax.ShapeDtypeStruct((steps * heads * tok_rows, head_dim), jnp.bfloat16)
+    in_vmem = pl.BlockSpec(memory_space=pltpu.VMEM)
+    pieces = pl.pallas_call(
         functools.partial(
             attend_kernel, steps, sections, heads, tok_rows, ctx_rows, head_dim, scale
         ),
-        out_shape=jax.ShapeDtypeStruct((peers, steps * heads * tok_rows, head_dim), jnp.bfloat16),
-        in_specs=[pl.BlockSpec(memory_space=pltpu.VMEM)],
-        out_specs=pl.BlockSpec(memory_space=pltpu.VMEM),
+        out_shape=[piece] * peers,
+        in_specs=[in_vmem],
+        out_specs=[in_vmem] * peers,
+        scratch_shapes=[pltpu.VMEM((peers,) + piece.shape, jnp.bfloat16)],
         compiler_params=pltpu.CompilerParams(vmem_limit_bytes=32 * 1024 * 1024),
     )(got)
-    back = lax.all_to_all(mixed, AXES, split_axis=0, concat_axis=0, tiled=True)
-    back = back.reshape(groups, steps, heads, tok_rows, head_dim).transpose(1, 3, 0, 2, 4)
-    return back.reshape(steps, 1, tok_rows, HEADS * head_dim)
+    came = [pieces[0]]
+    for offset in range(1, peers):
+        came.append(
+            lax.ppermute(pieces[offset], AXES, [(i, (i + offset) % peers) for i in range(peers)])
+        )
+    return pl.pallas_call(
+        functools.partial(place_kernel, steps, sections, heads, tok_rows, head_dim),
+        out_shape=jax.ShapeDtypeStruct((steps, 1, tok_rows, HEADS * head_dim), jnp.bfloat16),
+        in_specs=[in_vmem] * peers,
+        out_specs=in_vmem,
+        compiler_params=pltpu.CompilerParams(vmem_limit_bytes=32 * 1024 * 1024),
+    )(*came)
 
 
 def shards_copied(qkv_all, context_kv, sections, groups, copies, heads, scale):

time: 35.9 us -> 47.3 us (1.32)
  starting transfers between devices: 0 us -> 19.2 us
  blocking collectives: 31.8 us -> 21.6 us
  waiting for transfers between devices: 0 us -> 2.38 us
  Pallas kernels: 2.08 us -> 2.81 us
  local copies, waits for them, and re-layouts: 1.72 us -> 1.06 us
    ppermute x0 -> x15, starting transfers between devices: none -> 19.2 us  [shards(): lax.ppermute(pieces[offset], AXES, [(i, (i + offset) % peers) for i in ra...]
    all_to_all x1 -> x0, blocking collectives: 10.2 us -> none  [shards(): back = lax.all_to_all(mixed, AXES, split_axis=0, concat_axis=0, tiled=True)]
    ppermute x0 -> x15, waiting for transfers between devices: none -> 2.38 us  [shards(): lax.ppermute(pieces[offset], AXES, [(i, (i + offset) % peers) for i in ra...]
    pallas_call x0 -> x1, Pallas kernels: none -> 0.71 us  [shards(): pl.pallas_call(functools.partial(place_kernel, steps, sections, heads, to...]
    transpose x1 -> x0, local copies, waits for them, and re-layouts: 0.66 us -> none  [shards(): back.reshape(groups, steps, heads, tok_rows, head_dim)]
  transfers between devices with their start and end apart: 0 -> 15, of which waited for: 0 -> 2; matrix products, arithmetic and copies ran while one was open for 0% -> 0% of each run, Pallas kernels for 0% -> 0%
where the time goes in v2:
time: 47.3 us; the launch traced here: 47.1 us
  blocking collectives  21.6 us (46%)
  starting transfers between devices  19.2 us (41%)
  Pallas kernels  2.81 us (6%)
  waiting for transfers between devices  2.38 us (5%)
  local copies, waits for them, and re-layouts  1.06 us (2%)
    all_to_all x1, blocking collectives, shards(): got = lax.all_to_all(sent, AXES, split_axis=0, concat_axis=0, tiled=True)  21.6 us
    ppermute x15, starting transfers between devices, shards(): lax.ppermute(pieces[offset], AXES, [(i, (i + offset) % peers) for i in ra...  19.2 us
    ppermute x15, waiting for transfers between devices, shards(): lax.ppermute(pieces[offset], AXES, [(i, (i + offset) % peers) for i in ra...  2.38 us
    pallas_call x1, Pallas kernels, shards(): pl.pallas_call(functools.partial(attend_kernel, steps, sections, heads, t...  2.1 us
    another operation x1, local copies, waits for them, and re-layouts, shards(): blocks = qkv_all[:, 0].reshape(steps, tok_rows, groups, heads * 3, head_dim)  1.05 us
  transfers between devices with their start and end apart: 15, of which 2 were waited for; matrix products, arithmetic and copies ran while one was open for 0% of the time, Pallas kernels for 0%

profile of v2, /device:TPU:0, one launch (start us, length us, event | category | flops | bytes accessed | tf_op | source)
XLA Modules:
  0.0 47.1 jit_solution(10000120834374374195)
XLA Ops:
  0.0 0.0 copy-start
  0.0 1.1 %copy.3 = bf16[2,8,16,6,128]{4,1,3,0,2:T(8,128)(2,1)S(1)} copy(bf16[2,8,16,6,128]{4,1,3,2,0:T(8,128)(2,1)} %bitcast.10) | data formatting | bytes 786432 | tf_op jit(solution)/shard_map/reshape;squeeze | solution.py:92
  1.1 0.0 copy-done
  1.1 21.6 %all_to_all.5.got_ref = bf16[16,112,128]{2,1,0:T(8,128)(2,1)S(1)} all-to-all(bf16[16,112,128]{2,1,0:T(8,128)(2,1)S(1)} %pad_maximum_fusion), channel_id=1, replica_groups=mesh['rep'=2,'section'=2,'seq'=8] {'section','seq'}, dimensions={0} | all-to-all | bytes 917504 | tf_op jit(solution)/shard_map/all_to_all | solution.py:97
  22.7 2.1 %shard_map.28 = (bf16[32,128]{1,0:T(8,128)(2,1)S(1)}, bf16[32,128]{1,0:T(8,128)(2,1)S(1)}, bf16[32,128]{1,0:T(8,128)(2,1)S(1)}, bf16[32,128]{1,0:T(8,128)(2,1)S(...) custom-call(bf16[16,112,128]{2,1,0:T(8,128)(2,1)S(1)} %all_to_all.5., ...), custom_call_target="tpu_custom_call" | custom-call | tf_op jit(solution)/shard_map/pallas_call | solution.py:100
  24.8 0.6 %collective-permute-start = (bf16[32,128]{1,0:T(8,128)(2,1)S(1)}, bf16[32,128]{1,0:T(8,128)(2,1)S(1)}, u32[]{:S(2)}, u32[]{:S(2)}) collective-permute-start(bf16[32,128]{1,0:T(8,128)(2,1)S(1)} %get-tuple-element.22), channel_id=1, source_target_pairs={{0,1},{1,2},{2,3},{3,4},{4,5},{5,6},{6,7},{7,8},{8,9},{9,10},{10,1... | collective-permute-start | bytes 24584 | tf_op jit(solution)/shard_map/ppermute | solution.py:113
  25.4 0.9 %collective-permute-start.1 = (bf16[32,128]{1,0:T(8,128)(2,1)S(1)}, bf16[32,128]{1,0:T(8,128)(2,1)S(1)}, u32[]{:S(2)}, u32[]{:S(2)}) collective-permute-start(bf16[32,128]{1,0:T(8,128)(2,1)S(1)} %get-tuple-element.23), channel_id=1, source_target_pairs={{0,2},{1,3},{2,4},{3,5},{4,6},{5,7},{6,8},{7,9},{8,10},{9,11},{10,... | collective-permute-start | bytes 24584 | tf_op jit(solution)/shard_map/ppermute | solution.py:113
  26.3 1.7 %collective-permute-start.2 = (bf16[32,128]{1,0:T(8,128)(2,1)S(1)}, bf16[32,128]{1,0:T(8,128)(2,1)S(1)}, u32[]{:S(2)}, u32[]{:S(2)}) collective-permute-start(bf16[32,128]{1,0:T(8,128)(2,1)S(1)} %get-tuple-element.24), channel_id=1, source_target_pairs={{0,3},{1,4},{2,5},{3,6},{4,7},{5,8},{6,9},{7,10},{8,11},{9,12},{10... | collective-permute-start | bytes 24584 | tf_op jit(solution)/shard_map/ppermute | solution.py:113
  28.0 1.7 %collective-permute-start.3 = (bf16[32,128]{1,0:T(8,128)(2,1)S(1)}, bf16[32,128]{1,0:T(8,128)(2,1)S(1)}, u32[]{:S(2)}, u32[]{:S(2)}) collective-permute-start(bf16[32,128]{1,0:T(8,128)(2,1)S(1)} %get-tuple-element.25), channel_id=1, source_target_pairs={{0,4},{1,5},{2,6},{3,7},{4,8},{5,9},{6,10},{7,11},{8,12},{9,13},{1... | collective-permute-start | bytes 24584 | tf_op jit(solution)/shard_map/ppermute | solution.py:113
  29.7 0.0 collective-permute-start.4
  29.7 0.9 %collective-permute-done.refs_1_ = bf16[32,128]{1,0:T(8,128)(2,1)S(1)} collective-permute-done((bf16[32,128]{1,0:T(8,128)(2,1)S(1)}, bf16[32,128]{1,0:T(8,128)(2,1)S(1)}, u32[]{:S(2)}, u32[]{:S(2)}) %collective-permute-start) | collective-permute-done | bytes 8224 | tf_op jit(solution)/shard_map/ppermute | solution.py:113
  30.7 2.2 %collective-permute-start.5 = (bf16[32,128]{1,0:T(8,128)(2,1)S(1)}, bf16[32,128]{1,0:T(8,128)(2,1)S(1)}, u32[]{:S(2)}, u32[]{:S(2)}) collective-permute-start(bf16[32,128]{1,0:T(8,128)(2,1)S(1)} %get-tuple-element.27), channel_id=1, source_target_pairs={{0,6},{1,7},{2,8},{3,9},{4,10},{5,11},{6,12},{7,13},{8,14},{9,15},... | collective-permute-start | bytes 24584 | tf_op jit(solution)/shard_map/ppermute | solution.py:113
  32.9 0.0 collective-permute-done.1.refs_2_
  32.9 0.4 collective-permute-start.6
  33.3 0.0 collective-permute-done.2.refs_3_
  33.3 0.9 %collective-permute-start.7 = (bf16[32,128]{1,0:T(8,128)(2,1)S(1)}, bf16[32,128]{1,0:T(8,128)(2,1)S(1)}, u32[]{:S(2)}, u32[]{:S(2)}) collective-permute-start(bf16[32,128]{1,0:T(8,128)(2,1)S(1)} %get-tuple-element.29), channel_id=1, source_target_pairs={{0,8},{1,9},{2,10},{3,11},{4,12},{5,13},{6,14},{7,15},{8,0},{9,1},... | collective-permute-start | bytes 24584 | tf_op jit(solution)/shard_map/ppermute | solution.py:113
  34.2 0.0 collective-permute-done.3.refs_4_
  34.2 0.5 %collective-permute-start.8 = (bf16[32,128]{1,0:T(8,128)(2,1)S(1)}, bf16[32,128]{1,0:T(8,128)(2,1)S(1)}, u32[]{:S(2)}, u32[]{:S(2)}) collective-permute-start(bf16[32,128]{1,0:T(8,128)(2,1)S(1)} %get-tuple-element.30), channel_id=1, source_target_pairs={{0,9},{1,10},{2,11},{3,12},{4,13},{5,14},{6,15},{7,0},{8,1},{9,2},... | collective-permute-start | bytes 24584 | tf_op jit(solution)/shard_map/ppermute | solution.py:113
  34.7 0.0 collective-permute-done.4.refs_5_
  34.7 1.0 %collective-permute-start.9 = (bf16[32,128]{1,0:T(8,128)(2,1)S(1)}, bf16[32,128]{1,0:T(8,128)(2,1)S(1)}, u32[]{:S(2)}, u32[]{:S(2)}) collective-permute-start(bf16[32,128]{1,0:T(8,128)(2,1)S(1)} %get-tuple-element.31), channel_id=1, source_target_pairs={{0,10},{1,11},{2,12},{3,13},{4,14},{5,15},{6,0},{7,1},{8,2},{9,3},... | collective-permute-start | bytes 24584 | tf_op jit(solution)/shard_map/ppermute | solution.py:113
  35.7 0.0 collective-permute-done.5.refs_6_
  35.7 2.0 %collective-permute-start.10 = (bf16[32,128]{1,0:T(8,128)(2,1)S(1)}, bf16[32,128]{1,0:T(8,128)(2,1)S(1)}, u32[]{:S(2)}, u32[]{:S(2)}) collective-permute-start(bf16[32,128]{1,0:T(8,128)(2,1)S(1)} %get-tuple-element.32), channel_id=1, source_target_pairs={{0,11},{1,12},{2,13},{3,14},{4,15},{5,0},{6,1},{7,2},{8,3},{9,4},{... | collective-permute-start | bytes 24584 | tf_op jit(solution)/shard_map/ppermute | solution.py:113
  37.7 0.0 collective-permute-done.6.refs_7_
  37.7 2.4 %collective-permute-start.11 = (bf16[32,128]{1,0:T(8,128)(2,1)S(1)}, bf16[32,128]{1,0:T(8,128)(2,1)S(1)}, u32[]{:S(2)}, u32[]{:S(2)}) collective-permute-start(bf16[32,128]{1,0:T(8,128)(2,1)S(1)} %get-tuple-element.33), channel_id=1, source_target_pairs={{0,12},{1,13},{2,14},{3,15},{4,0},{5,1},{6,2},{7,3},{8,4},{9,5},{1... | collective-permute-start | bytes 24584 | tf_op jit(solution)/shard_map/ppermute | solution.py:113
  40.1 0.0 collective-permute-done.7.refs_8_
  40.1 0.4 collective-permute-start.12
  40.5 0.0 collective-permute-done.8.refs_9_
  40.5 2.3 %collective-permute-start.13 = (bf16[32,128]{1,0:T(8,128)(2,1)S(1)}, bf16[32,128]{1,0:T(8,128)(2,1)S(1)}, u32[]{:S(2)}, u32[]{:S(2)}) collective-permute-start(bf16[32,128]{1,0:T(8,128)(2,1)S(1)} %get-tuple-element.35), channel_id=1, source_target_pairs={{0,14},{1,15},{2,0},{3,1},{4,2},{5,3},{6,4},{7,5},{8,6},{9,7},{10,... | collective-permute-start | bytes 24584 | tf_op jit(solution)/shard_map/ppermute | solution.py:113
  42.8 0.0 collective-permute-done.9.refs_10_
  42.8 2.2 %collective-permute-start.14 = (bf16[32,128]{1,0:T(8,128)(2,1)S(1)}, bf16[32,128]{1,0:T(8,128)(2,1)S(1)}, u32[]{:S(2)}, u32[]{:S(2)}) collective-permute-start(bf16[32,128]{1,0:T(8,128)(2,1)S(1)} %get-tuple-element.36), channel_id=1, source_target_pairs={{0,15},{1,0},{2,1},{3,2},{4,3},{5,4},{6,5},{7,6},{8,7},{9,8},{10,9... | collective-permute-start | bytes 24584 | tf_op jit(solution)/shard_map/ppermute | solution.py:113
  45.0 0.0 collective-permute-done.10.refs_11_
  45.0 0.0 collective-permute-done.11.refs_12_
  45.0 0.0 collective-permute-done.12.refs_13_
  45.0 0.0 collective-permute-done.13.refs_14_
  45.0 1.4 %collective-permute-done.14.refs_15_ = bf16[32,128]{1,0:T(8,128)(2,1)S(1)} collective-permute-done((bf16[32,128]{1,0:T(8,128)(2,1)S(1)}, bf16[32,128]{1,0:T(8,128)(2,1)S(1)}, u32[]{:S(2)}, u32[]{:S(2)}) %collective-permute-start.14) | collective-permute-done | bytes 8224 | tf_op jit(solution)/shard_map/ppermute | solution.py:113
  46.4 0.7 %shard_map.29 = bf16[2,1,8,4096]{3,2,1,0:T(8,128)(2,1)} custom-call(bf16[32,128]{1,0:T(8,128)(2,1)S(1)} %get-tuple-element.21.refs_0_, bf16[32,128]{1,0:T(8,128)(2,1)S(1)} %collective-permute-done.refs_1_, bf16[32,128]{1,0:T(8,128)(2,1)S(1)} %collective-permute-done.1.refs_2_, bf16[32,128]{1,0:T(8,128)(2,1)S(1)} %collective-permute-done.2.refs_3_, ...), custom_call_target="tpu_custom_call" | custom-call | tf_op jit(solution)/shard_map/pallas_call | solution.py:115
  (1 shorter events, 0.0 us)
Async XLA Ops:
  0.0 1.1 %copy-start = (bf16[4,8192]{1,0:T(4,128)(2,1)S(1)}, bf16[4,8192]{1,0:T(4,128)(2,1)}, u32[]{:S(2)}) copy-start(bf16[4,8192]{1,0:T(4,128)(2,1)} %param.3) | copy-start | bytes 196612
  24.8 5.8 %collective-permute-start = (bf16[32,128]{1,0:T(8,128)(2,1)S(1)}, bf16[32,128]{1,0:T(8,128)(2,1)S(1)}, u32[]{:S(2)}, u32[]{:S(2)}) collective-permute-start(bf16[32,128]{1,0:T(8,128)(2,1)S(1)} %get-tuple-element.22), channel_id=1, source_target_pairs={{0,1},{1,2},{2,3},{3,4},{4,5},{5,6},{6,7},{7,8},{8,9},{9,10},{10,1... | collective-permute-start | bytes 24584 | tf_op jit(solution)/shard_map/ppermute | solution.py:113
  25.4 7.4 %collective-permute-start.1 = (bf16[32,128]{1,0:T(8,128)(2,1)S(1)}, bf16[32,128]{1,0:T(8,128)(2,1)S(1)}, u32[]{:S(2)}, u32[]{:S(2)}) collective-permute-start(bf16[32,128]{1,0:T(8,128)(2,1)S(1)} %get-tuple-element.23), channel_id=1, source_target_pairs={{0,2},{1,3},{2,4},{3,5},{4,6},{5,7},{6,8},{7,9},{8,10},{9,11},{10,... | collective-permute-start | bytes 24584 | tf_op jit(solution)/shard_map/ppermute | solution.py:113
  26.3 7.0 %collective-permute-start.2 = (bf16[32,128]{1,0:T(8,128)(2,1)S(1)}, bf16[32,128]{1,0:T(8,128)(2,1)S(1)}, u32[]{:S(2)}, u32[]{:S(2)}) collective-permute-start(bf16[32,128]{1,0:T(8,128)(2,1)S(1)} %get-tuple-element.24), channel_id=1, source_target_pairs={{0,3},{1,4},{2,5},{3,6},{4,7},{5,8},{6,9},{7,10},{8,11},{9,12},{10... | collective-permute-start | bytes 24584 | tf_op jit(solution)/shard_map/ppermute | solution.py:113
  28.0 6.1 %collective-permute-start.3 = (bf16[32,128]{1,0:T(8,128)(2,1)S(1)}, bf16[32,128]{1,0:T(8,128)(2,1)S(1)}, u32[]{:S(2)}, u32[]{:S(2)}) collective-permute-start(bf16[32,128]{1,0:T(8,128)(2,1)S(1)} %get-tuple-element.25), channel_id=1, source_target_pairs={{0,4},{1,5},{2,6},{3,7},{4,8},{5,9},{6,10},{7,11},{8,12},{9,13},{1... | collective-permute-start | bytes 24584 | tf_op jit(solution)/shard_map/ppermute | solution.py:113
  29.7 5.0 %collective-permute-start.4 = (bf16[32,128]{1,0:T(8,128)(2,1)S(1)}, bf16[32,128]{1,0:T(8,128)(2,1)S(1)}, u32[]{:S(2)}, u32[]{:S(2)}) collective-permute-start(bf16[32,128]{1,0:T(8,128)(2,1)S(1)} %get-tuple-element.26), channel_id=1, source_target_pairs={{0,5},{1,6},{2,7},{3,8},{4,9},{5,10},{6,11},{7,12},{8,13},{9,14},{... | collective-permute-start | bytes 24584 | tf_op jit(solution)/shard_map/ppermute | solution.py:113
  30.7 5.0 %collective-permute-start.5 = (bf16[32,128]{1,0:T(8,128)(2,1)S(1)}, bf16[32,128]{1,0:T(8,128)(2,1)S(1)}, u32[]{:S(2)}, u32[]{:S(2)}) collective-permute-start(bf16[32,128]{1,0:T(8,128)(2,1)S(1)} %get-tuple-element.27), channel_id=1, source_target_pairs={{0,6},{1,7},{2,8},{3,9},{4,10},{5,11},{6,12},{7,13},{8,14},{9,15},... | collective-permute-start | bytes 24584 | tf_op jit(solution)/shard_map/ppermute | solution.py:113
  32.9 4.8 %collective-permute-start.6 = (bf16[32,128]{1,0:T(8,128)(2,1)S(1)}, bf16[32,128]{1,0:T(8,128)(2,1)S(1)}, u32[]{:S(2)}, u32[]{:S(2)}) collective-permute-start(bf16[32,128]{1,0:T(8,128)(2,1)S(1)} %get-tuple-element.28), channel_id=1, source_target_pairs={{0,7},{1,8},{2,9},{3,10},{4,11},{5,12},{6,13},{7,14},{8,15},{9,0},... | collective-permute-start | bytes 24584 | tf_op jit(solution)/shard_map/ppermute | solution.py:113
  33.3 6.8 %collective-permute-start.7 = (bf16[32,128]{1,0:T(8,128)(2,1)S(1)}, bf16[32,128]{1,0:T(8,128)(2,1)S(1)}, u32[]{:S(2)}, u32[]{:S(2)}) collective-permute-start(bf16[32,128]{1,0:T(8,128)(2,1)S(1)} %get-tuple-element.29), channel_id=1, source_target_pairs={{0,8},{1,9},{2,10},{3,11},{4,12},{5,13},{6,14},{7,15},{8,0},{9,1},... | collective-permute-start | bytes 24584 | tf_op jit(solution)/shard_map/ppermute | solution.py:113
  34.2 6.4 %collective-permute-start.8 = (bf16[32,128]{1,0:T(8,128)(2,1)S(1)}, bf16[32,128]{1,0:T(8,128)(2,1)S(1)}, u32[]{:S(2)}, u32[]{:S(2)}) collective-permute-start(bf16[32,128]{1,0:T(8,128)(2,1)S(1)} %get-tuple-element.30), channel_id=1, source_target_pairs={{0,9},{1,10},{2,11},{3,12},{4,13},{5,14},{6,15},{7,0},{8,1},{9,2},... | collective-permute-start | bytes 24584 | tf_op jit(solution)/shard_map/ppermute | solution.py:113
  34.7 8.1 %collective-permute-start.9 = (bf16[32,128]{1,0:T(8,128)(2,1)S(1)}, bf16[32,128]{1,0:T(8,128)(2,1)S(1)}, u32[]{:S(2)}, u32[]{:S(2)}) collective-permute-start(bf16[32,128]{1,0:T(8,128)(2,1)S(1)} %get-tuple-element.31), channel_id=1, source_target_pairs={{0,10},{1,11},{2,12},{3,13},{4,14},{5,15},{6,0},{7,1},{8,2},{9,3},... | collective-permute-start | bytes 24584 | tf_op jit(solution)/shard_map/ppermute | solution.py:113
  35.7 9.3 %collective-permute-start.10 = (bf16[32,128]{1,0:T(8,128)(2,1)S(1)}, bf16[32,128]{1,0:T(8,128)(2,1)S(1)}, u32[]{:S(2)}, u32[]{:S(2)}) collective-permute-start(bf16[32,128]{1,0:T(8,128)(2,1)S(1)} %get-tuple-element.32), channel_id=1, source_target_pairs={{0,11},{1,12},{2,13},{3,14},{4,15},{5,0},{6,1},{7,2},{8,3},{9,4},{... | collective-permute-start | bytes 24584 | tf_op jit(solution)/shard_map/ppermute | solution.py:113
  37.7 7.3 %collective-permute-start.11 = (bf16[32,128]{1,0:T(8,128)(2,1)S(1)}, bf16[32,128]{1,0:T(8,128)(2,1)S(1)}, u32[]{:S(2)}, u32[]{:S(2)}) collective-permute-start(bf16[32,128]{1,0:T(8,128)(2,1)S(1)} %get-tuple-element.33), channel_id=1, source_target_pairs={{0,12},{1,13},{2,14},{3,15},{4,0},{5,1},{6,2},{7,3},{8,4},{9,5},{1... | collective-permute-start | bytes 24584 | tf_op jit(solution)/shard_map/ppermute | solution.py:113
  40.1 5.0 %collective-permute-start.12 = (bf16[32,128]{1,0:T(8,128)(2,1)S(1)}, bf16[32,128]{1,0:T(8,128)(2,1)S(1)}, u32[]{:S(2)}, u32[]{:S(2)}) collective-permute-start(bf16[32,128]{1,0:T(8,128)(2,1)S(1)} %get-tuple-element.34), channel_id=1, source_target_pairs={{0,13},{1,14},{2,15},{3,0},{4,1},{5,2},{6,3},{7,4},{8,5},{9,6},{10... | collective-permute-start | bytes 24584 | tf_op jit(solution)/shard_map/ppermute | solution.py:113
  40.5 4.5 %collective-permute-start.13 = (bf16[32,128]{1,0:T(8,128)(2,1)S(1)}, bf16[32,128]{1,0:T(8,128)(2,1)S(1)}, u32[]{:S(2)}, u32[]{:S(2)}) collective-permute-start(bf16[32,128]{1,0:T(8,128)(2,1)S(1)} %get-tuple-element.35), channel_id=1, source_target_pairs={{0,14},{1,15},{2,0},{3,1},{4,2},{5,3},{6,4},{7,5},{8,6},{9,7},{10,... | collective-permute-start | bytes 24584 | tf_op jit(solution)/shard_map/ppermute | solution.py:113
  42.8 3.7 %collective-permute-start.14 = (bf16[32,128]{1,0:T(8,128)(2,1)S(1)}, bf16[32,128]{1,0:T(8,128)(2,1)S(1)}, u32[]{:S(2)}, u32[]{:S(2)}) collective-permute-start(bf16[32,128]{1,0:T(8,128)(2,1)S(1)} %get-tuple-element.36), channel_id=1, source_target_pairs={{0,15},{1,0},{2,1},{3,2},{4,3},{5,4},{6,5},{7,6},{8,7},{9,8},{10,9... | collective-permute-start | bytes 24584 | tf_op jit(solution)/shard_map/ppermute | solution.py:113

commit v3 on v1

--- a/solution.py
+++ b/solution.py
@@ -1,4 +1,5 @@
 import functools
+import math
 
 import jax
 import jax.numpy as jnp
@@ -29,34 +30,83 @@
 ):
     sources = got_ref.shape[0]
     per_section = sources // sections
-    ctx_base = steps * heads * 3 * tok_rows
+    tokens = per_section * tok_rows
+    ctx_base = steps * heads * 3 * head_dim
+    log2_scale = scale * math.log2(math.e)
 
     def part(step, section, head, role):
-        base = ((step * heads + head) * 3 + role) * tok_rows
-        block = got_ref[section * per_section : (section + 1) * per_section, base : base + tok_rows]
-        return block.reshape(per_section * tok_rows, head_dim)
-
-    ctx_all = got_ref[:, ctx_base:]
+        base = ((step * heads + head) * 3 + role) * head_dim
+        rows = slice(section * per_section, (section + 1) * per_section)
+        return got_ref[rows, :, base : base + head_dim].reshape(tokens, head_dim)
 
     def context(head, role):
-        base = (head * 2 + role) * ctx_rows
-        return ctx_all[:, base : base + ctx_rows].reshape(sources * ctx_rows, head_dim)
-
+        base = ctx_base + role * head_dim
+        rows = slice(head * ctx_rows, (head + 1) * ctx_rows)
+        return got_ref[:, rows, base : base + head_dim].reshape(sources * ctx_rows, head_dim)
+
+    tasks = []
     for head in range(heads):
-        earlier_keys = [context(head, 0)]
-        earlier_vals = [context(head, 1)]
+        earlier = [(context(head, 0), context(head, 1))]
         for step in range(steps):
             own = [(part(step, s, head, 1), part(step, s, head, 2)) for s in range(sections)]
             for s in range(sections):
-                keys = jnp.concatenate(earlier_keys + [own[s][0]], axis=0)
-                vals = jnp.concatenate(earlier_vals + [own[s][1]], axis=0)
-                mixed = softmax_mix(part(step, s, head, 0), keys, vals, scale)
-                base = (step * heads + head) * tok_rows
-                out_ref[s * per_section : (s + 1) * per_section, base : base + tok_rows] = (
-                    mixed.reshape(per_section, tok_rows, head_dim)
+                pairs = earlier + [own[s]]
+                keys = jnp.concatenate([k for k, _ in pairs], axis=0)
+                vals = jnp.concatenate([v for _, v in pairs], axis=0)
+                tasks.append((step, s, head, part(step, s, head, 0), keys, vals))
+            earlier = earlier + [own[sections - 1]]
+    all_scores = [
+        lax.dot_general(q, k, (((1,), (1,)), ((), ())), preferred_element_type=jnp.float32)
+        for _, _, _, q, k, _ in tasks
+    ]
+    all_tops = [jnp.max(scores, axis=1, keepdims=True) for scores in all_scores]
+    all_weights = [
+        jnp.exp2((scores - top) * log2_scale).astype(jnp.bfloat16)
+        for scores, top in zip(all_scores, all_tops)
+    ]
+    all_mixed = [
+        jnp.dot(
+            weights,
+            jnp.concatenate([vals, jnp.ones_like(vals)], axis=1),
+            preferred_element_type=jnp.float32,
+        )
+        for weights, (_, _, _, _, _, vals) in zip(all_weights, tasks)
+    ]
+    for mixed, (step, s, head, _, _, _) in zip(all_mixed, tasks):
+        done = (mixed[:, :head_dim] / mixed[:, head_dim:]).astype(jnp.bfloat16)
+        base = (step * heads + head) * head_dim
+        out_ref[s * per_section : (s + 1) * per_section, :, base : base + head_dim] = done.reshape(
+            per_section, tok_rows, head_dim
+        )
+
+
+def pack_kernel(steps, groups, heads, ctx_rows, head_dim, qkv_ref, ctx_hbm, out_ref, ctx_ref, sems, ctx_sem):
+    ctx_copy = pltpu.make_async_copy(ctx_hbm, ctx_ref, ctx_sem)
+    ctx_copy.start()
+    width = heads * 3 * head_dim
+    copies = []
+    for step in range(steps):
+        for group in range(groups):
+            copies.append(
+                pltpu.make_async_copy(
+                    qkv_ref.at[step, 0, :, pl.ds(group * width, width)],
+                    out_ref.at[group, :, pl.ds(step * width, width)],
+                    sems.at[step, group],
                 )
-            earlier_keys.append(own[sections - 1][0])
-            earlier_vals.append(own[sections - 1][1])
+            )
+    for copy in copies:
+        copy.start()
+    base = steps * width
+    ctx_copy.wait()
+    for group in range(groups):
+        for role in range(2):
+            columns = [((group * heads + head) * 2 + role) * head_dim for head in range(heads)]
+            block = [ctx_ref[:, c : c + head_dim] for c in columns]
+            out_ref[group, :, base + role * head_dim : base + (role + 1) * head_dim] = (
+                jnp.concatenate(block, axis=0)
+            )
+    for copy in copies:
+        copy.wait()
 
 
 def shards(qkv_all, context_kv):
@@ -69,26 +119,37 @@
     head_dim = width // (3 * HEADS)
     ctx_rows = context_kv.shape[0]
     scale = head_dim ** (-0.5)
-    if copies > 1:
+    if copies > 1 or heads * ctx_rows != tok_rows:
         return shards_copied(qkv_all, context_kv, sections, groups, copies, heads, scale)
 
-    blocks = qkv_all[:, 0].reshape(steps, tok_rows, groups, heads * 3, head_dim)
-    blocks = blocks.transpose(2, 0, 3, 1, 4).reshape(groups, -1, head_dim)
-    ctx = context_kv.reshape(ctx_rows, groups, heads * 2, head_dim)
-    ctx = ctx.transpose(1, 2, 0, 3).reshape(groups, -1, head_dim)
-    sent = jnp.concatenate([blocks, ctx], axis=1)
+    in_vmem = pl.BlockSpec(memory_space=pltpu.VMEM)
+    params = pltpu.CompilerParams(vmem_limit_bytes=32 * 1024 * 1024)
+    sent = pl.pallas_call(
+        functools.partial(pack_kernel, steps, groups, heads, ctx_rows, head_dim),
+        out_shape=jax.ShapeDtypeStruct(
+            (groups, tok_rows, (steps * heads * 3 + 2) * head_dim), jnp.bfloat16
+        ),
+        in_specs=[pl.BlockSpec(memory_space=pltpu.HBM)] * 2,
+        out_specs=in_vmem,
+        scratch_shapes=[
+            pltpu.VMEM(context_kv.shape, jnp.bfloat16),
+            pltpu.SemaphoreType.DMA((steps, groups)),
+            pltpu.SemaphoreType.DMA,
+        ],
+        compiler_params=params,
+    )(*(pltpu.with_memory_space_constraint(x, pltpu.HBM) for x in (qkv_all, context_kv)))
     got = lax.all_to_all(sent, AXES, split_axis=0, concat_axis=0, tiled=True)
     mixed = pl.pallas_call(
         functools.partial(
             attend_kernel, steps, sections, heads, tok_rows, ctx_rows, head_dim, scale
         ),
-        out_shape=jax.ShapeDtypeStruct((peers, steps * heads * tok_rows, head_dim), jnp.bfloat16),
-        in_specs=[pl.BlockSpec(memory_space=pltpu.VMEM)],
-        out_specs=pl.BlockSpec(memory_space=pltpu.VMEM),
-        compiler_params=pltpu.CompilerParams(vmem_limit_bytes=32 * 1024 * 1024),
+        out_shape=jax.ShapeDtypeStruct((peers, tok_rows, steps * heads * head_dim), jnp.bfloat16),
+        in_specs=[in_vmem],
+        out_specs=in_vmem,
+        compiler_params=params,
     )(got)
     back = lax.all_to_all(mixed, AXES, split_axis=0, concat_axis=0, tiled=True)
-    back = back.reshape(groups, steps, heads, tok_rows, head_dim).transpose(1, 3, 0, 2, 4)
+    back = back.reshape(groups, tok_rows, steps, heads * head_dim).transpose(2, 1, 0, 3)
     return back.reshape(steps, 1, tok_rows, HEADS * head_dim)
 
 

time: 35.9 us -> 34.8 us (0.969)
  local copies, waits for them, and re-layouts: 1.72 us -> 0.66 us
    pallas_call x1, Pallas kernels: 2.08 us -> 0.57 us  [shards(): pl.pallas_call(functools.partial(attend_kernel, steps, sections, heads, t...]
    pallas_call x0 -> x1, Pallas kernels: none -> 1.43 us  [shards(): pl.pallas_call(functools.partial(pack_kernel, steps, groups, heads, ctx_r...]
    another operation x1 -> x0, local copies, waits for them, and re-layouts: 1.05 us -> none  [shards(): blocks = qkv_all[:, 0].reshape(steps, tok_rows, groups, heads * 3, head_dim)]
where the time goes in v3:
time: 34.8 us; the launch traced here: 34.5 us
  blocking collectives  31.8 us (91%)
  Pallas kernels  2 us (6%)
  local copies, waits for them, and re-layouts  0.66 us (2%)
    all_to_all x1, blocking collectives, shards(): got = lax.all_to_all(sent, AXES, split_axis=0, concat_axis=0, tiled=True)  21.6 us
    all_to_all x1, blocking collectives, shards(): back = lax.all_to_all(mixed, AXES, split_axis=0, concat_axis=0, tiled=True)  10.2 us
    pallas_call x1, Pallas kernels, shards(): pl.pallas_call(functools.partial(pack_kernel, steps, groups, heads, ctx_r...  1.43 us

profile of v3, /device:TPU:0, one launch (start us, length us, event | category | flops | bytes accessed | tf_op | source)
XLA Modules:
  0.0 34.5 jit_solution(4675097806178171591)
XLA Ops:
  0.0 1.4 %shard_map.28 = bf16[16,8,1792]{2,1,0:T(8,128)(2,1)S(1)} custom-call(bf16[2,1,8,12288]{3,2,1,0:T(8,128)(2,1)} %qkv_ref.1, bf16[4,8192]{1,0:T(4,128)(2,1)} %ctx_hbm.1), custom_call_target="tpu_custom_call" | custom-call | tf_op jit(solution)/shard_map/pallas_call | solution.py:127
  1.4 21.6 %all_to_all.10.got_ref = bf16[16,8,1792]{2,1,0:T(8,128)(2,1)S(1)} all-to-all(bf16[16,8,1792]{2,1,0:T(8,128)(2,1)S(1)} %shard_map.28), channel_id=1, replica_groups=mesh['rep'=2,'section'=2,'seq'=8] {'section','seq'}, dimensions={0} | all-to-all | bytes 917504 | tf_op jit(solution)/shard_map/all_to_all | solution.py:141
  23.0 0.6 %shard_map.29 = bf16[16,8,512]{2,1,0:T(8,128)(2,1)S(1)} custom-call(bf16[16,8,1792]{2,1,0:T(8,128)(2,1)S(1)} %all_to_all.10.got_ref), custom_call_target="tpu_custom_call" | custom-call | tf_op jit(solution)/shard_map/pallas_call | solution.py:142
  23.6 10.2 %all_to_all.11 = bf16[16,8,512]{2,1,0:T(8,128)(2,1)S(1)} all-to-all(bf16[16,8,512]{2,1,0:T(8,128)(2,1)S(1)} %shard_map.29), channel_id=1, replica_groups=mesh['rep'=2,'section'=2,'seq'=8] {'section','seq'}, dimensions={0} | all-to-all | bytes 262144 | tf_op jit(solution)/shard_map/all_to_all | solution.py:151
  33.8 0.7 %copy.3 = bf16[2,8,16,256]{3,1,2,0:T(8,128)(2,1)} copy(bf16[2,8,16,256]{3,1,0,2:T(8,128)(2,1)S(1)} %bitcast.4) | data formatting | bytes 262144 | tf_op jit(solution)/shard_map/transpose | solution.py:152

commit v4 on v3

--- a/solution.py
+++ b/solution.py
@@ -9,7 +9,7 @@
 from jax.sharding import PartitionSpec as P
 
 HEADS = 32
-AXES = ("section", "seq")
+AXES = ("seq", "section")
 
 
 def softmax_mix(queries, keys, values, scale):
@@ -28,21 +28,20 @@
 def attend_kernel(
     steps, sections, heads, tok_rows, ctx_rows, head_dim, scale, got_ref, out_ref
 ):
-    sources = got_ref.shape[0]
-    per_section = sources // sections
+    per_section = got_ref.shape[0]
+    sources = per_section * sections
     tokens = per_section * tok_rows
     ctx_base = steps * heads * 3 * head_dim
     log2_scale = scale * math.log2(math.e)
 
     def part(step, section, head, role):
         base = ((step * heads + head) * 3 + role) * head_dim
-        rows = slice(section * per_section, (section + 1) * per_section)
-        return got_ref[rows, :, base : base + head_dim].reshape(tokens, head_dim)
+        return got_ref[:, section, :, base : base + head_dim].reshape(tokens, head_dim)
 
     def context(head, role):
         base = ctx_base + role * head_dim
         rows = slice(head * ctx_rows, (head + 1) * ctx_rows)
-        return got_ref[:, rows, base : base + head_dim].reshape(sources * ctx_rows, head_dim)
+        return got_ref[:, :, rows, base : base + head_dim].reshape(sources * ctx_rows, head_dim)
 
     tasks = []
     for head in range(heads):
@@ -75,25 +74,29 @@
     for mixed, (step, s, head, _, _, _) in zip(all_mixed, tasks):
         done = (mixed[:, :head_dim] / mixed[:, head_dim:]).astype(jnp.bfloat16)
         base = (step * heads + head) * head_dim
-        out_ref[s * per_section : (s + 1) * per_section, :, base : base + head_dim] = done.reshape(
+        out_ref[:, s, :, base : base + head_dim] = done.reshape(
             per_section, tok_rows, head_dim
         )
 
 
-def pack_kernel(steps, groups, heads, ctx_rows, head_dim, qkv_ref, ctx_hbm, out_ref, ctx_ref, sems, ctx_sem):
+def pack_kernel(
+    steps, groups, heads, ctx_rows, head_dim, chunks, qkv_hbm, ctx_hbm, out_ref, qkv_ref, ctx_ref, sems, ctx_sem
+):
+    width = heads * 3 * head_dim
+    span = groups // chunks
     ctx_copy = pltpu.make_async_copy(ctx_hbm, ctx_ref, ctx_sem)
-    ctx_copy.start()
-    width = heads * 3 * head_dim
     copies = []
     for step in range(steps):
-        for group in range(groups):
+        for chunk in range(chunks):
+            columns = pl.ds(chunk * span * width, span * width)
             copies.append(
                 pltpu.make_async_copy(
-                    qkv_ref.at[step, 0, :, pl.ds(group * width, width)],
-                    out_ref.at[group, :, pl.ds(step * width, width)],
-                    sems.at[step, group],
+                    qkv_hbm.at[step, 0, :, columns],
+                    qkv_ref.at[step, :, columns],
+                    sems.at[step, chunk],
                 )
             )
+    ctx_copy.start()
     for copy in copies:
         copy.start()
     base = steps * width
@@ -105,8 +108,13 @@
             out_ref[group, :, base + role * head_dim : base + (role + 1) * head_dim] = (
                 jnp.concatenate(block, axis=0)
             )
-    for copy in copies:
-        copy.wait()
+    for step in range(steps):
+        for chunk in range(chunks):
+            copies[step * chunks + chunk].wait()
+            for group in range(chunk * span, (chunk + 1) * span):
+                out_ref[group, :, step * width : (step + 1) * width] = qkv_ref[
+                    step, :, group * width : (group + 1) * width
+                ]
 
 
 def shards(qkv_all, context_kv):
@@ -122,18 +130,20 @@
     if copies > 1 or heads * ctx_rows != tok_rows:
         return shards_copied(qkv_all, context_kv, sections, groups, copies, heads, scale)
 
+    chunks = math.gcd(groups, 2)
     in_vmem = pl.BlockSpec(memory_space=pltpu.VMEM)
     params = pltpu.CompilerParams(vmem_limit_bytes=32 * 1024 * 1024)
     sent = pl.pallas_call(
-        functools.partial(pack_kernel, steps, groups, heads, ctx_rows, head_dim),
+        functools.partial(pack_kernel, steps, groups, heads, ctx_rows, head_dim, chunks),
         out_shape=jax.ShapeDtypeStruct(
             (groups, tok_rows, (steps * heads * 3 + 2) * head_dim), jnp.bfloat16
         ),
         in_specs=[pl.BlockSpec(memory_space=pltpu.HBM)] * 2,
         out_specs=in_vmem,
         scratch_shapes=[
+            pltpu.VMEM((steps, tok_rows, width), jnp.bfloat16),
             pltpu.VMEM(context_kv.shape, jnp.bfloat16),
-            pltpu.SemaphoreType.DMA((steps, groups)),
+            pltpu.SemaphoreType.DMA((steps, chunks)),
             pltpu.SemaphoreType.DMA,
         ],
         compiler_params=params,
@@ -143,11 +153,14 @@
         functools.partial(
             attend_kernel, steps, sections, heads, tok_rows, ctx_rows, head_dim, scale
         ),
-        out_shape=jax.ShapeDtypeStruct((peers, tok_rows, steps * heads * head_dim), jnp.bfloat16),
+        out_shape=jax.ShapeDtypeStruct(
+            (peers // sections, sections, tok_rows, steps * heads * head_dim), jnp.bfloat16
+        ),
         in_specs=[in_vmem],
         out_specs=in_vmem,
         compiler_params=params,
-    )(got)
+    )(got.reshape((-1, sections) + got.shape[1:]))
+    mixed = mixed.reshape((peers,) + mixed.shape[2:])
     back = lax.all_to_all(mixed, AXES, split_axis=0, concat_axis=0, tiled=True)
     back = back.reshape(groups, tok_rows, steps, heads * head_dim).transpose(2, 1, 0, 3)
     return back.reshape(steps, 1, tok_rows, HEADS * head_dim)
@@ -173,10 +186,10 @@
     per_section = peers // sections
     cut = steps * heads * share
     end = cut + steps * heads * 2 * tok_rows
-    q = got[:, :cut].reshape(sections, per_section, steps, heads, share, head_dim)
-    q = q.transpose(2, 0, 3, 1, 4, 5).reshape(steps, sections, heads, -1, head_dim)
-    kv = got[:, cut:end].reshape(sections, per_section, steps, heads, 2, tok_rows, head_dim)
-    kv = kv.transpose(2, 0, 4, 3, 1, 5, 6).reshape(steps, sections, 2, heads, -1, head_dim)
+    q = got[:, :cut].reshape(per_section, sections, steps, heads, share, head_dim)
+    q = q.transpose(2, 1, 3, 0, 4, 5).reshape(steps, sections, heads, -1, head_dim)
+    kv = got[:, cut:end].reshape(per_section, sections, steps, heads, 2, tok_rows, head_dim)
+    kv = kv.transpose(2, 1, 4, 3, 0, 5, 6).reshape(steps, sections, 2, heads, -1, head_dim)
     ctx = got[:, end:].reshape(peers, heads, 2, ctx_rows, head_dim)
     earlier = [ctx.transpose(2, 1, 0, 3, 4).reshape(2, heads, -1, head_dim)]
     results = []
@@ -188,7 +201,7 @@
             )
         earlier = earlier + [kv[step, sections - 1]]
     mixed = jnp.stack(results).reshape(steps, sections, heads, per_section, share, head_dim)
-    mixed = mixed.transpose(1, 3, 0, 2, 4, 5).reshape(peers, -1, head_dim)
+    mixed = mixed.transpose(3, 1, 0, 2, 4, 5).reshape(peers, -1, head_dim)
     back = lax.all_to_all(mixed, AXES, split_axis=0, concat_axis=0, tiled=True)
     back = back.reshape(groups, copies, steps, heads, share, head_dim)
     back = back.transpose(2, 1, 4, 0, 3, 5)

time: 34.8 us -> 34.6 us (level)
    all_to_all x1, blocking collectives: 10.2 us -> 11.6 us  [shards(): back = lax.all_to_all(mixed, AXES, split_axis=0, concat_axis=0, tiled=True)]
    all_to_all x1, blocking collectives: 21.6 us -> 20.4 us  [shards(): got = lax.all_to_all(sent, AXES, split_axis=0, concat_axis=0, tiled=True)]
    reshape x0 -> x1, local copies, waits for them, and re-layouts: none -> 0.66 us  [shards(): back.reshape(groups, tok_rows, steps, heads * head_dim)]
    transpose x1 -> x0, local copies, waits for them, and re-layouts: 0.66 us -> none  [shards(): back.reshape(groups, tok_rows, steps, heads * head_dim)]
where the time goes in v4:
time: 34.6 us; the launch traced here: 34.4 us
  blocking collectives  32 us (92%)
  Pallas kernels  1.68 us (5%)
  local copies, waits for them, and re-layouts  0.66 us (2%)
    all_to_all x1, blocking collectives, shards(): got = lax.all_to_all(sent, AXES, split_axis=0, concat_axis=0, tiled=True)  20.4 us
    all_to_all x1, blocking collectives, shards(): back = lax.all_to_all(mixed, AXES, split_axis=0, concat_axis=0, tiled=True)  11.6 us
    pallas_call x1, Pallas kernels, shards(): pl.pallas_call(functools.partial(pack_kernel, steps, groups, heads, ctx_r...  1.11 us

profile of v4, /device:TPU:0, one launch (start us, length us, event | category | flops | bytes accessed | tf_op | source)
XLA Modules:
  0.0 34.4 jit_solution(361907237735693374)
XLA Ops:
  0.0 1.1 %shard_map.28 = bf16[16,8,1792]{2,1,0:T(8,128)(2,1)S(1)} custom-call(bf16[2,1,8,12288]{3,2,1,0:T(8,128)(2,1)} %qkv_hbm.1, bf16[4,8192]{1,0:T(4,128)(2,1)} %ctx_hbm.1), custom_call_target="tpu_custom_call" | custom-call | tf_op jit(solution)/shard_map/pallas_call | solution.py:136
  1.1 20.4 %all_to_all.10 = bf16[16,8,1792]{2,1,0:T(8,128)(2,1)S(1)} all-to-all(bf16[16,8,1792]{2,1,0:T(8,128)(2,1)S(1)} %shard_map.28), channel_id=1, replica_groups=mesh['rep'=2,'section'=2,'seq'=8] {'seq','section'}, dimensions={0} | all-to-all | bytes 917504 | tf_op jit(solution)/shard_map/all_to_all | solution.py:151
  21.5 0.6 %shard_map.29 = bf16[8,2,8,512]{3,2,1,0:T(8,128)(2,1)S(1)} custom-call(bf16[8,2,8,1792]{3,2,1,0:T(8,128)(2,1)S(1)} %bitcast.6), custom_call_target="tpu_custom_call" | custom-call | tf_op jit(solution)/shard_map/pallas_call | solution.py:152
  22.1 11.6 %all_to_all.11 = bf16[16,8,512]{2,1,0:T(8,128)(2,1)S(1)} all-to-all(bf16[16,8,512]{2,1,0:T(8,128)(2,1)S(1)} %bitcast.7), channel_id=1, replica_groups=mesh['rep'=2,'section'=2,'seq'=8] {'seq','section'}, dimensions={0} | all-to-all | bytes 262144 | tf_op jit(solution)/shard_map/all_to_all | solution.py:164
  33.7 0.7 %copy.3 = bf16[16,8,2,256]{3,1,0,2:T(8,128)(2,1)} copy(bf16[16,8,2,256]{3,1,2,0:T(8,128)(2,1)S(1)} %bitcast.8) | data formatting | bytes 262144 | tf_op jit(solution)/shard_map/reshape | solution.py:165

commit v5 on v4

--- a/solution.py
+++ b/solution.py
@@ -36,7 +36,7 @@
 
     def part(step, section, head, role):
         base = ((step * heads + head) * 3 + role) * head_dim
-        return got_ref[:, section, :, base : base + head_dim].reshape(tokens, head_dim)
+        return got_ref[:, sections - 1 - section, :, base : base + head_dim].reshape(tokens, head_dim)
 
     def context(head, role):
         base = ctx_base + role * head_dim
@@ -74,7 +74,7 @@
     for mixed, (step, s, head, _, _, _) in zip(all_mixed, tasks):
         done = (mixed[:, :head_dim] / mixed[:, head_dim:]).astype(jnp.bfloat16)
         base = (step * heads + head) * head_dim
-        out_ref[:, s, :, base : base + head_dim] = done.reshape(
+        out_ref[:, sections - 1 - s, :, base : base + head_dim] = done.reshape(
             per_section, tok_rows, head_dim
         )
 
@@ -148,7 +148,15 @@
         ],
         compiler_params=params,
     )(*(pltpu.with_memory_space_constraint(x, pltpu.HBM) for x in (qkv_all, context_kv)))
-    got = lax.all_to_all(sent, AXES, split_axis=0, concat_axis=0, tiled=True)
+    exchange = functools.partial(
+        lax.all_to_all,
+        axis_name=AXES,
+        split_axis=0,
+        concat_axis=0,
+        axis_index_groups=[list(range(peers - 1, -1, -1))],
+        tiled=True,
+    )
+    got = exchange(sent)
     mixed = pl.pallas_call(
         functools.partial(
             attend_kernel, steps, sections, heads, tok_rows, ctx_rows, head_dim, scale
@@ -161,7 +169,7 @@
         compiler_params=params,
     )(got.reshape((-1, sections) + got.shape[1:]))
     mixed = mixed.reshape((peers,) + mixed.shape[2:])
-    back = lax.all_to_all(mixed, AXES, split_axis=0, concat_axis=0, tiled=True)
+    back = exchange(mixed)
     back = back.reshape(groups, tok_rows, steps, heads * head_dim).transpose(2, 1, 0, 3)
     return back.reshape(steps, 1, tok_rows, HEADS * head_dim)
 

time: 34.6 us -> 31.2 us (0.902)
  blocking collectives: 32 us -> 28.6 us
    all_to_all x2, blocking collectives: 32 us -> 28.6 us  [the longest x1 19 us: shards(): got = exchange(sent)]
where the time goes in v5:
time: 31.2 us; the launch traced here: 31 us
  blocking collectives  28.6 us (92%)
  Pallas kernels  1.68 us (5%)
  local copies, waits for them, and re-layouts  0.66 us (2%)
    all_to_all x1, blocking collectives, shards(): got = exchange(sent)  19 us
    all_to_all x1, blocking collectives, shards(): back = exchange(mixed)  9.66 us
    pallas_call x1, Pallas kernels, shards(): pl.pallas_call(functools.partial(pack_kernel, steps, groups, heads, ctx_r...  1.11 us
    reshape x1, local copies, waits for them, and re-layouts, shards(): back.reshape(groups, tok_rows, steps, heads * head_dim)  0.66 us

profile of v5, /device:TPU:0, one launch (start us, length us, event | category | flops | bytes accessed | tf_op | source)
XLA Modules:
  0.0 31.0 jit_solution(14425360443181896533)
XLA Ops:
  0.0 1.1 %shard_map.28 = bf16[16,8,1792]{2,1,0:T(8,128)(2,1)S(1)} custom-call(bf16[2,1,8,12288]{3,2,1,0:T(8,128)(2,1)} %qkv_hbm.1, bf16[4,8192]{1,0:T(4,128)(2,1)} %ctx_hbm.1), custom_call_target="tpu_custom_call" | custom-call | tf_op jit(solution)/shard_map/pallas_call | solution.py:136
  1.1 19.0 %all_to_all.10 = bf16[16,8,1792]{2,1,0:T(8,128)(2,1)S(1)} all-to-all(bf16[16,8,1792]{2,1,0:T(8,128)(2,1)S(1)} %shard_map.28), channel_id=1, replica_groups={{15,7,14,6,13,5,12,4,11,3,10,2,9,1,8,0},{31,23,30,22,29,21,28,20,27,19,..., dimensions={0} | all-to-all | bytes 917504 | tf_op jit(solution)/shard_map/all_to_all | solution.py:159
  20.1 0.6 %shard_map.29 = bf16[8,2,8,512]{3,2,1,0:T(8,128)(2,1)S(1)} custom-call(bf16[8,2,8,1792]{3,2,1,0:T(8,128)(2,1)S(1)} %bitcast.6), custom_call_target="tpu_custom_call" | custom-call | tf_op jit(solution)/shard_map/pallas_call | solution.py:160
  20.7 9.7 %all_to_all.11 = bf16[16,8,512]{2,1,0:T(8,128)(2,1)S(1)} all-to-all(bf16[16,8,512]{2,1,0:T(8,128)(2,1)S(1)} %bitcast.7), channel_id=1, replica_groups={{15,7,14,6,13,5,12,4,11,3,10,2,9,1,8,0},{31,23,30,22,29,21,28,20,27,19,..., dimensions={0} | all-to-all | bytes 262144 | tf_op jit(solution)/shard_map/all_to_all | solution.py:172
  30.3 0.7 %copy.3 = bf16[16,8,2,256]{3,1,0,2:T(8,128)(2,1)} copy(bf16[16,8,2,256]{3,1,2,0:T(8,128)(2,1)S(1)} %bitcast.8) | data formatting | bytes 262144 | tf_op jit(solution)/shard_map/reshape | solution.py:173

commit v6 on v4

--- a/solution.py
+++ b/solution.py
@@ -26,22 +26,23 @@
 
 
 def attend_kernel(
-    steps, sections, heads, tok_rows, ctx_rows, head_dim, scale, got_ref, out_ref
+    steps, heads, tok_rows, ctx_rows, head_dim, scale, came_from, goes_to, got_ref, out_ref
 ):
-    per_section = got_ref.shape[0]
-    sources = per_section * sections
-    tokens = per_section * tok_rows
+    sections = len(came_from)
+    sources = got_ref.shape[0]
     ctx_base = steps * heads * 3 * head_dim
     log2_scale = scale * math.log2(math.e)
 
     def part(step, section, head, role):
         base = ((step * heads + head) * 3 + role) * head_dim
-        return got_ref[:, section, :, base : base + head_dim].reshape(tokens, head_dim)
+        return jnp.concatenate(
+            [got_ref[p, :, base : base + head_dim] for p in came_from[section]], axis=0
+        )
 
     def context(head, role):
         base = ctx_base + role * head_dim
         rows = slice(head * ctx_rows, (head + 1) * ctx_rows)
-        return got_ref[:, :, rows, base : base + head_dim].reshape(sources * ctx_rows, head_dim)
+        return got_ref[:, rows, base : base + head_dim].reshape(sources * ctx_rows, head_dim)
 
     tasks = []
     for head in range(heads):
@@ -74,14 +75,14 @@
     for mixed, (step, s, head, _, _, _) in zip(all_mixed, tasks):
         done = (mixed[:, :head_dim] / mixed[:, head_dim:]).astype(jnp.bfloat16)
         base = (step * heads + head) * head_dim
-        out_ref[:, s, :, base : base + head_dim] = done.reshape(
-            per_section, tok_rows, head_dim
-        )
+        for slot, p in enumerate(goes_to[s]):
+            out_ref[p, :, base : base + head_dim] = done[slot * tok_rows : (slot + 1) * tok_rows]
 
 
 def pack_kernel(
-    steps, groups, heads, ctx_rows, head_dim, chunks, qkv_hbm, ctx_hbm, out_ref, qkv_ref, ctx_ref, sems, ctx_sem
+    steps, block_of, heads, ctx_rows, head_dim, chunks, qkv_hbm, ctx_hbm, out_ref, qkv_ref, ctx_ref, sems, ctx_sem
 ):
+    groups = len(block_of)
     width = heads * 3 * head_dim
     span = groups // chunks
     ctx_copy = pltpu.make_async_copy(ctx_hbm, ctx_ref, ctx_sem)
@@ -105,16 +106,36 @@
         for role in range(2):
             columns = [((group * heads + head) * 2 + role) * head_dim for head in range(heads)]
             block = [ctx_ref[:, c : c + head_dim] for c in columns]
-            out_ref[group, :, base + role * head_dim : base + (role + 1) * head_dim] = (
+            out_ref[block_of[group], :, base + role * head_dim : base + (role + 1) * head_dim] = (
                 jnp.concatenate(block, axis=0)
             )
     for step in range(steps):
         for chunk in range(chunks):
             copies[step * chunks + chunk].wait()
             for group in range(chunk * span, (chunk + 1) * span):
-                out_ref[group, :, step * width : (step + 1) * width] = qkv_ref[
+                out_ref[block_of[group], :, step * width : (step + 1) * width] = qkv_ref[
                     step, :, group * width : (group + 1) * width
                 ]
+
+
+def exchange(blocks, order):
+    return lax.all_to_all(
+        blocks, AXES, split_axis=0, concat_axis=0, axis_index_groups=[order], tiled=True
+    )
+
+
+def send_orders(sections, per_section):
+    peers = sections * per_section
+    quarter = math.gcd(peers, 4)
+    row = peers // quarter
+    rows = ([3, 1, 0, 2] if quarter == 4 else list(range(quarter)))
+    first = [z * row + i for z in rows for i in range(row - 1, -1, -1)]
+    second = [
+        seq * sections + s
+        for s in range(sections - 1, -1, -1)
+        for seq in range(per_section - 1, -1, -1)
+    ]
+    return first, second
 
 
 def shards(qkv_all, context_kv):
@@ -131,10 +152,16 @@
         return shards_copied(qkv_all, context_kv, sections, groups, copies, heads, scale)
 
     chunks = math.gcd(groups, 2)
+    per_section = peers // sections
+    first, second = send_orders(sections, per_section)
+    devices = range(sections * per_section)
+    block_of = [first.index(second[group]) for group in range(groups)]
+    came_from = [[first.index(d) for d in devices if d % sections == s] for s in range(sections)]
+    goes_to = [[second.index(d) for d in devices if d % sections == s] for s in range(sections)]
     in_vmem = pl.BlockSpec(memory_space=pltpu.VMEM)
     params = pltpu.CompilerParams(vmem_limit_bytes=32 * 1024 * 1024)
     sent = pl.pallas_call(
-        functools.partial(pack_kernel, steps, groups, heads, ctx_rows, head_dim, chunks),
+        functools.partial(pack_kernel, steps, block_of, heads, ctx_rows, head_dim, chunks),
         out_shape=jax.ShapeDtypeStruct(
             (groups, tok_rows, (steps * heads * 3 + 2) * head_dim), jnp.bfloat16
         ),
@@ -148,20 +175,17 @@
         ],
         compiler_params=params,
     )(*(pltpu.with_memory_space_constraint(x, pltpu.HBM) for x in (qkv_all, context_kv)))
-    got = lax.all_to_all(sent, AXES, split_axis=0, concat_axis=0, tiled=True)
+    got = exchange(sent, first)
     mixed = pl.pallas_call(
         functools.partial(
-            attend_kernel, steps, sections, heads, tok_rows, ctx_rows, head_dim, scale
+            attend_kernel, steps, heads, tok_rows, ctx_rows, head_dim, scale, came_from, goes_to
         ),
-        out_shape=jax.ShapeDtypeStruct(
-            (peers // sections, sections, tok_rows, steps * heads * head_dim), jnp.bfloat16
-        ),
+        out_shape=jax.ShapeDtypeStruct((peers, tok_rows, steps * heads * head_dim), jnp.bfloat16),
         in_specs=[in_vmem],
         out_specs=in_vmem,
         compiler_params=params,
-    )(got.reshape((-1, sections) + got.shape[1:]))
-    mixed = mixed.reshape((peers,) + mixed.shape[2:])
-    back = lax.all_to_all(mixed, AXES, split_axis=0, concat_axis=0, tiled=True)
+    )(got)
+    back = exchange(mixed, second)
     back = back.reshape(groups, tok_rows, steps, heads * head_dim).transpose(2, 1, 0, 3)
     return back.reshape(steps, 1, tok_rows, HEADS * head_dim)
 

time: 34.6 us -> 31.5 us (0.910)
  blocking collectives: 32 us -> 28.9 us
    all_to_all x2, blocking collectives: 32 us -> 28.9 us  [exchange(): lax.all_to_all(blocks, AXES, split_axis=0, concat_axis=0, axis_index_grou...]
    reshape x1 -> x0, local copies, waits for them, and re-layouts: 0.66 us -> none  [shards(): back.reshape(groups, tok_rows, steps, heads * head_dim)]
    transpose x0 -> x1, local copies, waits for them, and re-layouts: none -> 0.66 us  [shards(): back.reshape(groups, tok_rows, steps, heads * head_dim)]
where the time goes in v6:
time: 31.5 us; the launch traced here: 31.3 us
  blocking collectives  28.9 us (92%)
  Pallas kernels  1.68 us (5%)
  local copies, waits for them, and re-layouts  0.66 us (2%)
    all_to_all x2, blocking collectives, exchange(): lax.all_to_all(blocks, AXES, split_axis=0, concat_axis=0, axis_index_grou...  28.9 us
    pallas_call x1, Pallas kernels, shards(): pl.pallas_call(functools.partial(pack_kernel, steps, block_of, heads, ctx...  1.11 us
    transpose x1, local copies, waits for them, and re-layouts, shards(): back.reshape(groups, tok_rows, steps, heads * head_dim)  0.66 us

profile of v6, /device:TPU:0, one launch (start us, length us, event | category | flops | bytes accessed | tf_op | source)
XLA Modules:
  0.0 31.3 jit_solution(17267684547564443670)
XLA Ops:
  0.0 1.1 %shard_map.28 = bf16[16,8,1792]{2,1,0:T(8,128)(2,1)S(1)} custom-call(bf16[2,1,8,12288]{3,2,1,0:T(8,128)(2,1)} %qkv_hbm.1, bf16[4,8192]{1,0:T(4,128)(2,1)} %ctx_hbm.1), custom_call_target="tpu_custom_call" | custom-call | tf_op jit(solution)/shard_map/pallas_call | solution.py:163
  1.1 19.4 %all_to_all.10.got_ref = bf16[16,8,1792]{2,1,0:T(8,128)(2,1)S(1)} all-to-all(bf16[16,8,1792]{2,1,0:T(8,128)(2,1)S(1)} %shard_map.28), channel_id=1, replica_groups={{15,7,14,6,11,3,10,2,9,1,8,0,13,5,12,4},{31,23,30,22,27,19,26,18,25,17,..., dimensions={0} | all-to-all | bytes 917504 | tf_op jit(solution)/shard_map/all_to_all | solution.py:122
  20.5 0.6 %shard_map.29 = bf16[16,8,512]{2,1,0:T(8,128)(2,1)S(1)} custom-call(bf16[16,8,1792]{2,1,0:T(8,128)(2,1)S(1)} %all_to_all.10.got_ref), custom_call_target="tpu_custom_call" | custom-call | tf_op jit(solution)/shard_map/pallas_call | solution.py:179
  21.1 9.6 %all_to_all.11 = bf16[16,8,512]{2,1,0:T(8,128)(2,1)S(1)} all-to-all(bf16[16,8,512]{2,1,0:T(8,128)(2,1)S(1)} %shard_map.29), channel_id=1, replica_groups={{15,14,13,12,11,10,9,8,7,6,5,4,3,2,1,0},{31,30,29,28,27,26,25,24,23,22,..., dimensions={0} | all-to-all | bytes 262144 | tf_op jit(solution)/shard_map/all_to_all | solution.py:122
  30.6 0.7 %copy.3 = bf16[2,8,16,256]{3,1,2,0:T(8,128)(2,1)} copy(bf16[2,8,16,256]{3,1,0,2:T(8,128)(2,1)S(1)} %bitcast.4) | data formatting | bytes 262144 | tf_op jit(solution)/shard_map/transpose | solution.py:189

commit v7 on v6

--- a/solution.py
+++ b/solution.py
@@ -128,13 +128,8 @@
     peers = sections * per_section
     quarter = math.gcd(peers, 4)
     row = peers // quarter
-    rows = ([3, 1, 0, 2] if quarter == 4 else list(range(quarter)))
-    first = [z * row + i for z in rows for i in range(row - 1, -1, -1)]
-    second = [
-        seq * sections + s
-        for s in range(sections - 1, -1, -1)
-        for seq in range(per_section - 1, -1, -1)
-    ]
+    first = [z * row + i for i in range(row - 1, -1, -1) for z in range(quarter - 1, -1, -1)]
+    second = first
     return first, second
 
 

time: 31.5 us -> 32.2 us (1.022)
  blocking collectives: 28.9 us -> 29.6 us
    all_to_all x2, blocking collectives: 28.9 us -> 29.6 us  [exchange(): lax.all_to_all(blocks, AXES, split_axis=0, concat_axis=0, axis_index_grou...]
where the time goes in v7:
time: 32.2 us; the launch traced here: 31.9 us
  blocking collectives  29.6 us (92%)
  Pallas kernels  1.68 us (5%)
  local copies, waits for them, and re-layouts  0.66 us (2%)
    all_to_all x2, blocking collectives, exchange(): lax.all_to_all(blocks, AXES, split_axis=0, concat_axis=0, axis_index_grou...  29.6 us
    pallas_call x1, Pallas kernels, shards(): pl.pallas_call(functools.partial(pack_kernel, steps, block_of, heads, ctx...  1.11 us
    transpose x1, local copies, waits for them, and re-layouts, shards(): back.reshape(groups, tok_rows, steps, heads * head_dim)  0.66 us

profile of v7, /device:TPU:0, one launch (start us, length us, event | category | flops | bytes accessed | tf_op | source)
XLA Modules:
  0.0 31.9 jit_solution(10211613892649874246)
XLA Ops:
  0.0 1.1 %shard_map.28 = bf16[16,8,1792]{2,1,0:T(8,128)(2,1)S(1)} custom-call(bf16[2,1,8,12288]{3,2,1,0:T(8,128)(2,1)} %qkv_hbm.1, bf16[4,8192]{1,0:T(4,128)(2,1)} %ctx_hbm.1), custom_call_target="tpu_custom_call" | custom-call | tf_op jit(solution)/shard_map/pallas_call | solution.py:158
  1.1 19.5 %all_to_all.10.got_ref = bf16[16,8,1792]{2,1,0:T(8,128)(2,1)S(1)} all-to-all(bf16[16,8,1792]{2,1,0:T(8,128)(2,1)S(1)} %shard_map.28), channel_id=1, replica_groups={{15,13,11,9,7,5,3,1,14,12,10,8,6,4,2,0},{31,29,27,25,23,21,19,17,30,28,..., dimensions={0} | all-to-all | bytes 917504 | tf_op jit(solution)/shard_map/all_to_all | solution.py:122
  20.6 0.6 %shard_map.29 = bf16[16,8,512]{2,1,0:T(8,128)(2,1)S(1)} custom-call(bf16[16,8,1792]{2,1,0:T(8,128)(2,1)S(1)} %all_to_all.10.got_ref), custom_call_target="tpu_custom_call" | custom-call | tf_op jit(solution)/shard_map/pallas_call | solution.py:174
  21.2 10.1 %all_to_all.11 = bf16[16,8,512]{2,1,0:T(8,128)(2,1)S(1)} all-to-all(bf16[16,8,512]{2,1,0:T(8,128)(2,1)S(1)} %shard_map.29), channel_id=1, replica_groups={{15,13,11,9,7,5,3,1,14,12,10,8,6,4,2,0},{31,29,27,25,23,21,19,17,30,28,..., dimensions={0} | all-to-all | bytes 262144 | tf_op jit(solution)/shard_map/all_to_all | solution.py:122
  31.3 0.7 %copy.3 = bf16[2,8,16,256]{3,1,2,0:T(8,128)(2,1)} copy(bf16[2,8,16,256]{3,1,0,2:T(8,128)(2,1)S(1)} %bitcast.4) | data formatting | bytes 262144 | tf_op jit(solution)/shard_map/transpose | solution.py:184

commit v8 on v7

--- a/solution.py
+++ b/solution.py
@@ -128,8 +128,9 @@
     peers = sections * per_section
     quarter = math.gcd(peers, 4)
     row = peers // quarter
-    first = [z * row + i for i in range(row - 1, -1, -1) for z in range(quarter - 1, -1, -1)]
-    second = first
+    turned = [z * row + i for z in range(quarter - 1, -1, -1) for i in range(row - 1, -1, -1)]
+    first = turned[row:] + turned[:row]
+    second = turned[peers // 2 :] + turned[: peers // 2]
     return first, second
 
 

time: 32.2 us -> 30 us (0.932)
  blocking collectives: 29.6 us -> 27.4 us
    all_to_all x2, blocking collectives: 29.6 us -> 27.4 us  [exchange(): lax.all_to_all(blocks, AXES, split_axis=0, concat_axis=0, axis_index_grou...]
where the time goes in v8:
time: 30 us; the launch traced here: 29.7 us
  blocking collectives  27.4 us (91%)
  Pallas kernels  1.68 us (6%)
  local copies, waits for them, and re-layouts  0.66 us (2%)
    all_to_all x2, blocking collectives, exchange(): lax.all_to_all(blocks, AXES, split_axis=0, concat_axis=0, axis_index_grou...  27.4 us
    pallas_call x1, Pallas kernels, shards(): pl.pallas_call(functools.partial(pack_kernel, steps, block_of, heads, ctx...  1.11 us
    transpose x1, local copies, waits for them, and re-layouts, shards(): back.reshape(groups, tok_rows, steps, heads * head_dim)  0.66 us

profile of v8, /device:TPU:0, one launch (start us, length us, event | category | flops | bytes accessed | tf_op | source)
XLA Modules:
  0.0 29.7 jit_solution(10363143741441625842)
XLA Ops:
  0.0 1.1 %shard_map.28 = bf16[16,8,1792]{2,1,0:T(8,128)(2,1)S(1)} custom-call(bf16[2,1,8,12288]{3,2,1,0:T(8,128)(2,1)} %qkv_hbm.1, bf16[4,8192]{1,0:T(4,128)(2,1)} %ctx_hbm.1), custom_call_target="tpu_custom_call" | custom-call | tf_op jit(solution)/shard_map/pallas_call | solution.py:159
  1.1 18.0 %all_to_all.10.got_ref = bf16[16,8,1792]{2,1,0:T(8,128)(2,1)S(1)} all-to-all(bf16[16,8,1792]{2,1,0:T(8,128)(2,1)S(1)} %shard_map.28), channel_id=1, replica_groups={{13,5,12,4,11,3,10,2,9,1,8,0,15,7,14,6},{29,21,28,20,27,19,26,18,25,17,..., dimensions={0} | all-to-all | bytes 917504 | tf_op jit(solution)/shard_map/all_to_all | solution.py:122
  19.1 0.6 %shard_map.29 = bf16[16,8,512]{2,1,0:T(8,128)(2,1)S(1)} custom-call(bf16[16,8,1792]{2,1,0:T(8,128)(2,1)S(1)} %all_to_all.10.got_ref), custom_call_target="tpu_custom_call" | custom-call | tf_op jit(solution)/shard_map/pallas_call | solution.py:175
  19.7 9.4 %all_to_all.11 = bf16[16,8,512]{2,1,0:T(8,128)(2,1)S(1)} all-to-all(bf16[16,8,512]{2,1,0:T(8,128)(2,1)S(1)} %shard_map.29), channel_id=1, replica_groups={{11,3,10,2,9,1,8,0,15,7,14,6,13,5,12,4},{27,19,26,18,25,17,24,16,31,23,..., dimensions={0} | all-to-all | bytes 262144 | tf_op jit(solution)/shard_map/all_to_all | solution.py:122
  29.1 0.7 %copy.3 = bf16[2,8,16,256]{3,1,2,0:T(8,128)(2,1)} copy(bf16[2,8,16,256]{3,1,0,2:T(8,128)(2,1)S(1)} %bitcast.4) | data formatting | bytes 262144 | tf_op jit(solution)/shard_map/transpose | solution.py:185

commit v9 on v8

--- a/solution.py
+++ b/solution.py
@@ -129,8 +129,8 @@
     quarter = math.gcd(peers, 4)
     row = peers // quarter
     turned = [z * row + i for z in range(quarter - 1, -1, -1) for i in range(row - 1, -1, -1)]
-    first = turned[row:] + turned[:row]
-    second = turned[peers // 2 :] + turned[: peers // 2]
+    first = turned[row + 1 :] + turned[: row + 1]
+    second = turned[row:] + turned[:row]
     return first, second
 
 

time: 30 us -> 30.2 us (level)
  no operation moved by 1% of the time
where the time goes in v9:
time: 30.2 us; the launch traced here: 30 us
  blocking collectives  27.7 us (92%)
  Pallas kernels  1.68 us (6%)
  local copies, waits for them, and re-layouts  0.66 us (2%)
    all_to_all x2, blocking collectives, exchange(): lax.all_to_all(blocks, AXES, split_axis=0, concat_axis=0, axis_index_grou...  27.7 us
    pallas_call x1, Pallas kernels, shards(): pl.pallas_call(functools.partial(pack_kernel, steps, block_of, heads, ctx...  1.11 us
    transpose x1, local copies, waits for them, and re-layouts, shards(): back.reshape(groups, tok_rows, steps, heads * head_dim)  0.66 us

profile of v9, /device:TPU:0, one launch (start us, length us, event | category | flops | bytes accessed | tf_op | source)
XLA Modules:
  0.0 30.0 jit_solution(14489169858127571527)
XLA Ops:
  0.0 1.1 %shard_map.28 = bf16[16,8,1792]{2,1,0:T(8,128)(2,1)S(1)} custom-call(bf16[2,1,8,12288]{3,2,1,0:T(8,128)(2,1)} %qkv_hbm.1, bf16[4,8192]{1,0:T(4,128)(2,1)} %ctx_hbm.1), custom_call_target="tpu_custom_call" | custom-call | tf_op jit(solution)/shard_map/pallas_call | solution.py:159
  1.1 18.8 %all_to_all.10.got_ref = bf16[16,8,1792]{2,1,0:T(8,128)(2,1)S(1)} all-to-all(bf16[16,8,1792]{2,1,0:T(8,128)(2,1)S(1)} %shard_map.28), channel_id=1, replica_groups={{5,12,4,11,3,10,2,9,1,8,0,15,7,14,6,13},{21,28,20,27,19,26,18,25,17,24,..., dimensions={0} | all-to-all | bytes 917504 | tf_op jit(solution)/shard_map/all_to_all | solution.py:122
  20.0 0.6 %shard_map.29 = bf16[16,8,512]{2,1,0:T(8,128)(2,1)S(1)} custom-call(bf16[16,8,1792]{2,1,0:T(8,128)(2,1)S(1)} %all_to_all.10.got_ref), custom_call_target="tpu_custom_call" | custom-call | tf_op jit(solution)/shard_map/pallas_call | solution.py:175
  20.5 8.8 %all_to_all.11 = bf16[16,8,512]{2,1,0:T(8,128)(2,1)S(1)} all-to-all(bf16[16,8,512]{2,1,0:T(8,128)(2,1)S(1)} %shard_map.29), channel_id=1, replica_groups={{13,5,12,4,11,3,10,2,9,1,8,0,15,7,14,6},{29,21,28,20,27,19,26,18,25,17,..., dimensions={0} | all-to-all | bytes 262144 | tf_op jit(solution)/shard_map/all_to_all | solution.py:122
  29.4 0.7 %copy.3 = bf16[2,8,16,256]{3,1,2,0:T(8,128)(2,1)} copy(bf16[2,8,16,256]{3,1,0,2:T(8,128)(2,1)S(1)} %bitcast.4) | data formatting | bytes 262144 | tf_op jit(solution)/shard_map/transpose | solution.py:185

commit v10 on v9

--- a/solution.py
+++ b/solution.py
@@ -129,8 +129,10 @@
     quarter = math.gcd(peers, 4)
     row = peers // quarter
     turned = [z * row + i for z in range(quarter - 1, -1, -1) for i in range(row - 1, -1, -1)]
-    first = turned[row + 1 :] + turned[: row + 1]
-    second = turned[row:] + turned[:row]
+    half = peers // 2
+    first = turned[half:] + turned[:half]
+    half += row // 2
+    second = turned[half:] + turned[:half]
     return first, second
 
 

time: 30.2 us -> 31.2 us (1.033)
  blocking collectives: 27.7 us -> 28.6 us
    all_to_all x2, blocking collectives: 27.7 us -> 28.6 us  [exchange(): lax.all_to_all(blocks, AXES, split_axis=0, concat_axis=0, axis_index_grou...]
where the time goes in v10:
time: 31.2 us; the launch traced here: 31 us
  blocking collectives  28.6 us (92%)
  Pallas kernels  1.68 us (5%)
  local copies, waits for them, and re-layouts  0.66 us (2%)
    all_to_all x2, blocking collectives, exchange(): lax.all_to_all(blocks, AXES, split_axis=0, concat_axis=0, axis_index_grou...  28.6 us
    pallas_call x1, Pallas kernels, shards(): pl.pallas_call(functools.partial(pack_kernel, steps, block_of, heads, ctx...  1.11 us
    transpose x1, local copies, waits for them, and re-layouts, shards(): back.reshape(groups, tok_rows, steps, heads * head_dim)  0.66 us

profile of v10, /device:TPU:0, one launch (start us, length us, event | category | flops | bytes accessed | tf_op | source)
XLA Modules:
  0.0 31.0 jit_solution(6992783257061421691)
XLA Ops:
  0.0 1.1 %shard_map.28 = bf16[16,8,1792]{2,1,0:T(8,128)(2,1)S(1)} custom-call(bf16[2,1,8,12288]{3,2,1,0:T(8,128)(2,1)} %qkv_hbm.1, bf16[4,8192]{1,0:T(4,128)(2,1)} %ctx_hbm.1), custom_call_target="tpu_custom_call" | custom-call | tf_op jit(solution)/shard_map/pallas_call | solution.py:161
  1.1 19.3 %all_to_all.10.got_ref = bf16[16,8,1792]{2,1,0:T(8,128)(2,1)S(1)} all-to-all(bf16[16,8,1792]{2,1,0:T(8,128)(2,1)S(1)} %shard_map.28), channel_id=1, replica_groups={{11,3,10,2,9,1,8,0,15,7,14,6,13,5,12,4},{27,19,26,18,25,17,24,16,31,23,..., dimensions={0} | all-to-all | bytes 917504 | tf_op jit(solution)/shard_map/all_to_all | solution.py:122
  20.4 0.6 %shard_map.29 = bf16[16,8,512]{2,1,0:T(8,128)(2,1)S(1)} custom-call(bf16[16,8,1792]{2,1,0:T(8,128)(2,1)S(1)} %all_to_all.10.got_ref), custom_call_target="tpu_custom_call" | custom-call | tf_op jit(solution)/shard_map/pallas_call | solution.py:177
  20.9 9.4 %all_to_all.11 = bf16[16,8,512]{2,1,0:T(8,128)(2,1)S(1)} all-to-all(bf16[16,8,512]{2,1,0:T(8,128)(2,1)S(1)} %shard_map.29), channel_id=1, replica_groups={{10,2,9,1,8,0,15,7,14,6,13,5,12,4,11,3},{26,18,25,17,24,16,31,23,30,22,..., dimensions={0} | all-to-all | bytes 262144 | tf_op jit(solution)/shard_map/all_to_all | solution.py:122
  30.3 0.7 %copy.3 = bf16[2,8,16,256]{3,1,2,0:T(8,128)(2,1)} copy(bf16[2,8,16,256]{3,1,0,2:T(8,128)(2,1)S(1)} %bitcast.4) | data formatting | bytes 262144 | tf_op jit(solution)/shard_map/transpose | solution.py:187

commit v11 on v8

--- a/solution.py
+++ b/solution.py
@@ -130,7 +130,9 @@
     row = peers // quarter
     turned = [z * row + i for z in range(quarter - 1, -1, -1) for i in range(row - 1, -1, -1)]
     first = turned[row:] + turned[:row]
-    second = turned[peers // 2 :] + turned[: peers // 2]
+    half = quarter // 2
+    rows = list(range(half, quarter)) + list(range(half))
+    second = [z * row + i for z in rows for i in range(row - 1, -1, -1)]
     return first, second
 
 

time: 30 us -> 29.1 us (0.970)
  blocking collectives: 27.4 us -> 26.4 us
    all_to_all x2, blocking collectives: 27.4 us -> 26.4 us  [exchange(): lax.all_to_all(blocks, AXES, split_axis=0, concat_axis=0, axis_index_grou...]
where the time goes in v11:
time: 29.1 us; the launch traced here: 28.7 us
  blocking collectives  26.4 us (91%)
  Pallas kernels  1.68 us (6%)
  local copies, waits for them, and re-layouts  0.66 us (2%)
    all_to_all x2, blocking collectives, exchange(): lax.all_to_all(blocks, AXES, split_axis=0, concat_axis=0, axis_index_grou...  26.4 us
    pallas_call x1, Pallas kernels, shards(): pl.pallas_call(functools.partial(pack_kernel, steps, block_of, heads, ctx...  1.11 us
    transpose x1, local copies, waits for them, and re-layouts, shards(): back.reshape(groups, tok_rows, steps, heads * head_dim)  0.66 us

profile of v11, /device:TPU:0, one launch (start us, length us, event | category | flops | bytes accessed | tf_op | source)
XLA Modules:
  0.0 28.7 jit_solution(7673944698693225841)
XLA Ops:
  0.0 1.1 %shard_map.28 = bf16[16,8,1792]{2,1,0:T(8,128)(2,1)S(1)} custom-call(bf16[2,1,8,12288]{3,2,1,0:T(8,128)(2,1)} %qkv_hbm.1, bf16[4,8192]{1,0:T(4,128)(2,1)} %ctx_hbm.1), custom_call_target="tpu_custom_call" | custom-call | tf_op jit(solution)/shard_map/pallas_call | solution.py:161
  1.1 18.0 %all_to_all.10.got_ref = bf16[16,8,1792]{2,1,0:T(8,128)(2,1)S(1)} all-to-all(bf16[16,8,1792]{2,1,0:T(8,128)(2,1)S(1)} %shard_map.28), channel_id=1, replica_groups={{13,5,12,4,11,3,10,2,9,1,8,0,15,7,14,6},{29,21,28,20,27,19,26,18,25,17,..., dimensions={0} | all-to-all | bytes 917504 | tf_op jit(solution)/shard_map/all_to_all | solution.py:122
  19.1 0.6 %shard_map.29 = bf16[16,8,512]{2,1,0:T(8,128)(2,1)S(1)} custom-call(bf16[16,8,1792]{2,1,0:T(8,128)(2,1)S(1)} %all_to_all.10.got_ref), custom_call_target="tpu_custom_call" | custom-call | tf_op jit(solution)/shard_map/pallas_call | solution.py:177
  19.7 8.4 %all_to_all.11 = bf16[16,8,512]{2,1,0:T(8,128)(2,1)S(1)} all-to-all(bf16[16,8,512]{2,1,0:T(8,128)(2,1)S(1)} %shard_map.29), channel_id=1, replica_groups={{13,5,12,4,15,7,14,6,9,1,8,0,11,3,10,2},{29,21,28,20,31,23,30,22,25,17,..., dimensions={0} | all-to-all | bytes 262144 | tf_op jit(solution)/shard_map/all_to_all | solution.py:122
  28.1 0.7 %copy.3 = bf16[2,8,16,256]{3,1,2,0:T(8,128)(2,1)} copy(bf16[2,8,16,256]{3,1,0,2:T(8,128)(2,1)S(1)} %bitcast.4) | data formatting | bytes 262144 | tf_op jit(solution)/shard_map/transpose | solution.py:187

commit v12 on v7

--- a/solution.py
+++ b/solution.py
@@ -118,6 +118,24 @@
                 ]
 
 
+def unpack_kernel(back_ref, out_hbm, rows_ref, sems):
+    groups = back_ref.shape[0]
+    steps = rows_ref.shape[0]
+    width = rows_ref.shape[2] // groups
+    copies = []
+    for step in range(steps):
+        for group in range(groups):
+            rows_ref[step, :, group * width : (group + 1) * width] = back_ref[
+                group, :, step * width : (step + 1) * width
+            ]
+        copies.append(
+            pltpu.make_async_copy(rows_ref.at[step], out_hbm.at[step, 0], sems.at[step])
+        )
+        copies[-1].start()
+    for copy in copies:
+        copy.wait()
+
+
 def exchange(blocks, order):
     return lax.all_to_all(
         blocks, AXES, split_axis=0, concat_axis=0, axis_index_groups=[order], tiled=True
@@ -128,7 +146,9 @@
     peers = sections * per_section
     quarter = math.gcd(peers, 4)
     row = peers // quarter
-    first = [z * row + i for i in range(row - 1, -1, -1) for z in range(quarter - 1, -1, -1)]
+    half = quarter // 2
+    rows = list(range(half, quarter)) + list(range(half))
+    first = [z * row + i for z in rows for i in range(row - 1, -1, -1)]
     second = first
     return first, second
 
@@ -146,7 +166,7 @@
     if copies > 1 or heads * ctx_rows != tok_rows:
         return shards_copied(qkv_all, context_kv, sections, groups, copies, heads, scale)
 
-    chunks = math.gcd(groups, 2)
+    chunks = math.gcd(groups, 4)
     per_section = peers // sections
     first, second = send_orders(sections, per_section)
     devices = range(sections * per_section)
@@ -181,8 +201,17 @@
         compiler_params=params,
     )(got)
     back = exchange(mixed, second)
-    back = back.reshape(groups, tok_rows, steps, heads * head_dim).transpose(2, 1, 0, 3)
-    return back.reshape(steps, 1, tok_rows, HEADS * head_dim)
+    return pl.pallas_call(
+        unpack_kernel,
+        out_shape=jax.ShapeDtypeStruct((steps, 1, tok_rows, HEADS * head_dim), jnp.bfloat16),
+        in_specs=[in_vmem],
+        out_specs=pl.BlockSpec(memory_space=pltpu.HBM),
+        scratch_shapes=[
+            pltpu.VMEM((steps, tok_rows, HEADS * head_dim), jnp.bfloat16),
+            pltpu.SemaphoreType.DMA((steps,)),
+        ],
+        compiler_params=params,
+    )(back)
 
 
 def shards_copied(qkv_all, context_kv, sections, groups, copies, heads, scale):

time: 32.2 us -> 29.4 us (0.913)
  blocking collectives: 29.6 us -> 26.5 us
  Pallas kernels: 1.68 us -> 2.39 us
  local copies, waits for them, and re-layouts: 0.66 us -> 0 us
    all_to_all x2, blocking collectives: 29.6 us -> 26.5 us  [exchange(): lax.all_to_all(blocks, AXES, split_axis=0, concat_axis=0, axis_index_grou...]
    pallas_call x0 -> x1, Pallas kernels: none -> 0.67 us  [shards(): pl.pallas_call(unpack_kernel, out_shape=jax.ShapeDtypeStruct((steps, 1, t...]
    transpose x1 -> x0, local copies, waits for them, and re-layouts: 0.66 us -> none  [shards(): back.reshape(groups, tok_rows, steps, heads * head_dim)]
where the time goes in v12:
time: 29.4 us; the launch traced here: 28.9 us
  blocking collectives  26.5 us (90%)
  Pallas kernels  2.39 us (8%)
    all_to_all x2, blocking collectives, exchange(): lax.all_to_all(blocks, AXES, split_axis=0, concat_axis=0, axis_index_grou...  26.5 us
    pallas_call x1, Pallas kernels, shards(): pl.pallas_call(functools.partial(pack_kernel, steps, block_of, heads, ctx...  1.15 us
    pallas_call x1, Pallas kernels, shards(): pl.pallas_call(unpack_kernel, out_shape=jax.ShapeDtypeStruct((steps, 1, t...  0.67 us

profile of v12, /device:TPU:0, one launch (start us, length us, event | category | flops | bytes accessed | tf_op | source)
XLA Modules:
  0.0 28.9 jit_solution(1859060773476617584)
XLA Ops:
  0.0 1.1 %shard_map.28 = bf16[16,8,1792]{2,1,0:T(8,128)(2,1)S(1)} custom-call(bf16[2,1,8,12288]{3,2,1,0:T(8,128)(2,1)} %qkv_hbm.1, bf16[4,8192]{1,0:T(4,128)(2,1)} %ctx_hbm.1), custom_call_target="tpu_custom_call" | custom-call | tf_op jit(solution)/shard_map/pallas_call | solution.py:178
  1.2 16.8 %all_to_all.10.got_ref = bf16[16,8,1792]{2,1,0:T(8,128)(2,1)S(1)} all-to-all(bf16[16,8,1792]{2,1,0:T(8,128)(2,1)S(1)} %shard_map.28), channel_id=1, replica_groups={{13,5,12,4,15,7,14,6,9,1,8,0,11,3,10,2},{29,21,28,20,31,23,30,22,25,17,..., dimensions={0} | all-to-all | bytes 917504 | tf_op jit(solution)/shard_map/all_to_all | solution.py:140
  17.9 0.6 %shard_map.29 = bf16[16,8,512]{2,1,0:T(8,128)(2,1)S(1)} custom-call(bf16[16,8,1792]{2,1,0:T(8,128)(2,1)S(1)} %all_to_all.10.got_ref), custom_call_target="tpu_custom_call" | custom-call | tf_op jit(solution)/shard_map/pallas_call | solution.py:194
  18.5 9.7 %all_to_all.11.back_ref = bf16[16,8,512]{2,1,0:T(8,128)(2,1)S(1)} all-to-all(bf16[16,8,512]{2,1,0:T(8,128)(2,1)S(1)} %shard_map.29), channel_id=1, replica_groups={{13,5,12,4,15,7,14,6,9,1,8,0,11,3,10,2},{29,21,28,20,31,23,30,22,25,17,..., dimensions={0} | all-to-all | bytes 262144 | tf_op jit(solution)/shard_map/all_to_all | solution.py:140
  28.3 0.7 %shard_map.30 = bf16[2,1,8,4096]{3,2,1,0:T(8,128)(2,1)} custom-call(bf16[16,8,512]{2,1,0:T(8,128)(2,1)S(1)} %all_to_all.11.back_ref), custom_call_target="tpu_custom_call" | custom-call | tf_op jit(solution)/shard_map/pallas_call | solution.py:204

commit v13 on v11

--- a/solution.py
+++ b/solution.py
@@ -128,11 +128,12 @@
     peers = sections * per_section
     quarter = math.gcd(peers, 4)
     row = peers // quarter
-    turned = [z * row + i for z in range(quarter - 1, -1, -1) for i in range(row - 1, -1, -1)]
+    inner = [i for s in range(sections - 1, -1, -1) for i in range(row - sections + s, -1, -sections)]
+    turned = [z * row + i for z in range(quarter - 1, -1, -1) for i in inner]
     first = turned[row:] + turned[:row]
     half = quarter // 2
     rows = list(range(half, quarter)) + list(range(half))
-    second = [z * row + i for z in rows for i in range(row - 1, -1, -1)]
+    second = [z * row + i for z in rows for i in inner]
     return first, second
 
 

time: 29.1 us -> 30.1 us (1.034)
  blocking collectives: 26.4 us -> 27.5 us
    all_to_all x2, blocking collectives: 26.4 us -> 27.5 us  [exchange(): lax.all_to_all(blocks, AXES, split_axis=0, concat_axis=0, axis_index_grou...]
where the time goes in v13:
time: 30.1 us; the launch traced here: 29.9 us
  blocking collectives  27.5 us (91%)
  Pallas kernels  1.68 us (6%)
  local copies, waits for them, and re-layouts  0.66 us (2%)
    all_to_all x2, blocking collectives, exchange(): lax.all_to_all(blocks, AXES, split_axis=0, concat_axis=0, axis_index_grou...  27.5 us
    pallas_call x1, Pallas kernels, shards(): pl.pallas_call(functools.partial(pack_kernel, steps, block_of, heads, ctx...  1.11 us
    transpose x1, local copies, waits for them, and re-layouts, shards(): back.reshape(groups, tok_rows, steps, heads * head_dim)  0.66 us

profile of v13, /device:TPU:0, one launch (start us, length us, event | category | flops | bytes accessed | tf_op | source)
XLA Modules:
  0.0 29.9 jit_solution(16136164319799497575)
XLA Ops:
  0.0 1.1 %shard_map.28 = bf16[16,8,1792]{2,1,0:T(8,128)(2,1)S(1)} custom-call(bf16[2,1,8,12288]{3,2,1,0:T(8,128)(2,1)} %qkv_hbm.1, bf16[4,8192]{1,0:T(4,128)(2,1)} %ctx_hbm.1), custom_call_target="tpu_custom_call" | custom-call | tf_op jit(solution)/shard_map/pallas_call | solution.py:162
  1.1 18.3 %all_to_all.10.got_ref = bf16[16,8,1792]{2,1,0:T(8,128)(2,1)S(1)} all-to-all(bf16[16,8,1792]{2,1,0:T(8,128)(2,1)S(1)} %shard_map.28), channel_id=1, replica_groups={{13,12,5,4,11,10,3,2,9,8,1,0,15,14,7,6},{29,28,21,20,27,26,19,18,25,24,..., dimensions={0} | all-to-all | bytes 917504 | tf_op jit(solution)/shard_map/all_to_all | solution.py:122
  19.4 0.6 %shard_map.29 = bf16[16,8,512]{2,1,0:T(8,128)(2,1)S(1)} custom-call(bf16[16,8,1792]{2,1,0:T(8,128)(2,1)S(1)} %all_to_all.10.got_ref), custom_call_target="tpu_custom_call" | custom-call | tf_op jit(solution)/shard_map/pallas_call | solution.py:178
  20.0 9.2 %all_to_all.11 = bf16[16,8,512]{2,1,0:T(8,128)(2,1)S(1)} all-to-all(bf16[16,8,512]{2,1,0:T(8,128)(2,1)S(1)} %shard_map.29), channel_id=1, replica_groups={{13,12,5,4,15,14,7,6,9,8,1,0,11,10,3,2},{29,28,21,20,31,30,23,22,25,24,..., dimensions={0} | all-to-all | bytes 262144 | tf_op jit(solution)/shard_map/all_to_all | solution.py:122
  29.2 0.7 %copy.3 = bf16[2,8,16,256]{3,1,2,0:T(8,128)(2,1)} copy(bf16[2,8,16,256]{3,1,0,2:T(8,128)(2,1)S(1)} %bitcast.4) | data formatting | bytes 262144 | tf_op jit(solution)/shard_map/transpose | solution.py:188

commit v14 on v11

--- a/solution.py
+++ b/solution.py
@@ -128,10 +128,11 @@
     peers = sections * per_section
     quarter = math.gcd(peers, 4)
     row = peers // quarter
-    turned = [z * row + i for z in range(quarter - 1, -1, -1) for i in range(row - 1, -1, -1)]
-    first = turned[row:] + turned[:row]
     half = quarter // 2
     rows = list(range(half, quarter)) + list(range(half))
+    across = rows[::half] + rows[1::half] if quarter == 4 else rows
+    first = [z * row + i for z in across for i in range(row - 1, -1, -1)]
+    rows = rows[:half] + rows[: half - 1 : -1]
     second = [z * row + i for z in rows for i in range(row - 1, -1, -1)]
     return first, second
 

time: 29.1 us -> 30 us (1.031)
  blocking collectives: 26.4 us -> 27.4 us
    all_to_all x2, blocking collectives: 26.4 us -> 27.4 us  [exchange(): lax.all_to_all(blocks, AXES, split_axis=0, concat_axis=0, axis_index_grou...]
where the time goes in v14:
time: 30 us; the launch traced here: 29.8 us
  blocking collectives  27.4 us (91%)
  Pallas kernels  1.68 us (6%)
  local copies, waits for them, and re-layouts  0.66 us (2%)
    all_to_all x2, blocking collectives, exchange(): lax.all_to_all(blocks, AXES, split_axis=0, concat_axis=0, axis_index_grou...  27.4 us
    pallas_call x1, Pallas kernels, shards(): pl.pallas_call(functools.partial(pack_kernel, steps, block_of, heads, ctx...  1.11 us
    transpose x1, local copies, waits for them, and re-layouts, shards(): back.reshape(groups, tok_rows, steps, heads * head_dim)  0.66 us

profile of v14, /device:TPU:0, one launch (start us, length us, event | category | flops | bytes accessed | tf_op | source)
XLA Modules:
  0.0 29.8 jit_solution(16845893312385090355)
XLA Ops:
  0.0 1.1 %shard_map.28 = bf16[16,8,1792]{2,1,0:T(8,128)(2,1)S(1)} custom-call(bf16[2,1,8,12288]{3,2,1,0:T(8,128)(2,1)} %qkv_hbm.1, bf16[4,8192]{1,0:T(4,128)(2,1)} %ctx_hbm.1), custom_call_target="tpu_custom_call" | custom-call | tf_op jit(solution)/shard_map/pallas_call | solution.py:162
  1.1 16.8 %all_to_all.10.got_ref = bf16[16,8,1792]{2,1,0:T(8,128)(2,1)S(1)} all-to-all(bf16[16,8,1792]{2,1,0:T(8,128)(2,1)S(1)} %shard_map.28), channel_id=1, replica_groups={{13,5,12,4,9,1,8,0,15,7,14,6,11,3,10,2},{29,21,28,20,25,17,24,16,31,23,..., dimensions={0} | all-to-all | bytes 917504 | tf_op jit(solution)/shard_map/all_to_all | solution.py:122
  17.9 0.6 %shard_map.29 = bf16[16,8,512]{2,1,0:T(8,128)(2,1)S(1)} custom-call(bf16[16,8,1792]{2,1,0:T(8,128)(2,1)S(1)} %all_to_all.10.got_ref), custom_call_target="tpu_custom_call" | custom-call | tf_op jit(solution)/shard_map/pallas_call | solution.py:178
  18.5 10.6 %all_to_all.11 = bf16[16,8,512]{2,1,0:T(8,128)(2,1)S(1)} all-to-all(bf16[16,8,512]{2,1,0:T(8,128)(2,1)S(1)} %shard_map.29), channel_id=1, replica_groups={{13,5,12,4,15,7,14,6,11,3,10,2,9,1,8,0},{29,21,28,20,31,23,30,22,27,19,..., dimensions={0} | all-to-all | bytes 262144 | tf_op jit(solution)/shard_map/all_to_all | solution.py:122
  29.1 0.7 %copy.3 = bf16[2,8,16,256]{3,1,2,0:T(8,128)(2,1)} copy(bf16[2,8,16,256]{3,1,0,2:T(8,128)(2,1)S(1)} %bitcast.4) | data formatting | bytes 262144 | tf_op jit(solution)/shard_map/transpose | solution.py:188

commit v15 on v14

--- a/solution.py
+++ b/solution.py
@@ -131,9 +131,9 @@
     half = quarter // 2
     rows = list(range(half, quarter)) + list(range(half))
     across = rows[::half] + rows[1::half] if quarter == 4 else rows
-    first = [z * row + i for z in across for i in range(row - 1, -1, -1)]
-    rows = rows[:half] + rows[: half - 1 : -1]
-    second = [z * row + i for z in rows for i in range(row - 1, -1, -1)]
+    inner = [i for i in range(row) if i % 2][::-1] + [i for i in range(row) if i % 2 == 0]
+    first = [z * row + i for z in across for i in inner]
+    second = [z * row + i for z in rows for i in inner]
     return first, second
 
 

time: 30 us -> 30.1 us (level)
  no operation moved by 1% of the time
where the time goes in v15:
time: 30.1 us; the launch traced here: 29.9 us
  blocking collectives  27.5 us (91%)
  Pallas kernels  1.68 us (6%)
  local copies, waits for them, and re-layouts  0.66 us (2%)
    all_to_all x2, blocking collectives, exchange(): lax.all_to_all(blocks, AXES, split_axis=0, concat_axis=0, axis_index_grou...  27.5 us
    pallas_call x1, Pallas kernels, shards(): pl.pallas_call(functools.partial(pack_kernel, steps, block_of, heads, ctx...  1.11 us
    transpose x1, local copies, waits for them, and re-layouts, shards(): back.reshape(groups, tok_rows, steps, heads * head_dim)  0.66 us

profile of v15, /device:TPU:0, one launch (start us, length us, event | category | flops | bytes accessed | tf_op | source)
XLA Modules:
  0.0 29.9 jit_solution(5914094437092050795)
XLA Ops:
  0.0 1.1 %shard_map.28 = bf16[16,8,1792]{2,1,0:T(8,128)(2,1)S(1)} custom-call(bf16[2,1,8,12288]{3,2,1,0:T(8,128)(2,1)} %qkv_hbm.1, bf16[4,8192]{1,0:T(4,128)(2,1)} %ctx_hbm.1), custom_call_target="tpu_custom_call" | custom-call | tf_op jit(solution)/shard_map/pallas_call | solution.py:162
  1.1 17.2 %all_to_all.10.got_ref = bf16[16,8,1792]{2,1,0:T(8,128)(2,1)S(1)} all-to-all(bf16[16,8,1792]{2,1,0:T(8,128)(2,1)S(1)} %shard_map.28), channel_id=1, replica_groups={{13,12,4,5,9,8,0,1,15,14,6,7,11,10,2,3},{29,28,20,21,25,24,16,17,31,30,..., dimensions={0} | all-to-all | bytes 917504 | tf_op jit(solution)/shard_map/all_to_all | solution.py:122
  18.3 0.6 %shard_map.29 = bf16[16,8,512]{2,1,0:T(8,128)(2,1)S(1)} custom-call(bf16[16,8,1792]{2,1,0:T(8,128)(2,1)S(1)} %all_to_all.10.got_ref), custom_call_target="tpu_custom_call" | custom-call | tf_op jit(solution)/shard_map/pallas_call | solution.py:178
  18.9 10.3 %all_to_all.11 = bf16[16,8,512]{2,1,0:T(8,128)(2,1)S(1)} all-to-all(bf16[16,8,512]{2,1,0:T(8,128)(2,1)S(1)} %shard_map.29), channel_id=1, replica_groups={{13,12,4,5,15,14,6,7,9,8,0,1,11,10,2,3},{29,28,20,21,31,30,22,23,25,24,..., dimensions={0} | all-to-all | bytes 262144 | tf_op jit(solution)/shard_map/all_to_all | solution.py:122
  29.2 0.7 %copy.3 = bf16[2,8,16,256]{3,1,2,0:T(8,128)(2,1)} copy(bf16[2,8,16,256]{3,1,0,2:T(8,128)(2,1)S(1)} %bitcast.4) | data formatting | bytes 262144 | tf_op jit(solution)/shard_map/transpose | solution.py:188

commit v16 on v14

--- a/solution.py
+++ b/solution.py
@@ -132,7 +132,6 @@
     rows = list(range(half, quarter)) + list(range(half))
     across = rows[::half] + rows[1::half] if quarter == 4 else rows
     first = [z * row + i for z in across for i in range(row - 1, -1, -1)]
-    rows = rows[:half] + rows[: half - 1 : -1]
     second = [z * row + i for z in rows for i in range(row - 1, -1, -1)]
     return first, second
 

time: 30 us -> 29.9 us (level)
    all_to_all x2, blocking collectives: 27.4 us -> 27.1 us  [exchange(): lax.all_to_all(blocks, AXES, split_axis=0, concat_axis=0, axis_index_grou...]
where the time goes in v16:
time: 29.9 us; the launch traced here: 29.4 us
  blocking collectives  27.1 us (91%)
  Pallas kernels  1.68 us (6%)
  local copies, waits for them, and re-layouts  0.66 us (2%)
    all_to_all x2, blocking collectives, exchange(): lax.all_to_all(blocks, AXES, split_axis=0, concat_axis=0, axis_index_grou...  27.1 us
    pallas_call x1, Pallas kernels, shards(): pl.pallas_call(functools.partial(pack_kernel, steps, block_of, heads, ctx...  1.11 us
    transpose x1, local copies, waits for them, and re-layouts, shards(): back.reshape(groups, tok_rows, steps, heads * head_dim)  0.66 us

profile of v16, /device:TPU:0, one launch (start us, length us, event | category | flops | bytes accessed | tf_op | source)
XLA Modules:
  0.0 29.4 jit_solution(14175072889200521713)
XLA Ops:
  0.0 1.1 %shard_map.28 = bf16[16,8,1792]{2,1,0:T(8,128)(2,1)S(1)} custom-call(bf16[2,1,8,12288]{3,2,1,0:T(8,128)(2,1)} %qkv_hbm.1, bf16[4,8192]{1,0:T(4,128)(2,1)} %ctx_hbm.1), custom_call_target="tpu_custom_call" | custom-call | tf_op jit(solution)/shard_map/pallas_call | solution.py:161
  1.1 16.8 %all_to_all.10.got_ref = bf16[16,8,1792]{2,1,0:T(8,128)(2,1)S(1)} all-to-all(bf16[16,8,1792]{2,1,0:T(8,128)(2,1)S(1)} %shard_map.28), channel_id=1, replica_groups={{13,5,12,4,9,1,8,0,15,7,14,6,11,3,10,2},{29,21,28,20,25,17,24,16,31,23,..., dimensions={0} | all-to-all | bytes 917504 | tf_op jit(solution)/shard_map/all_to_all | solution.py:122
  17.9 0.6 %shard_map.29 = bf16[16,8,512]{2,1,0:T(8,128)(2,1)S(1)} custom-call(bf16[16,8,1792]{2,1,0:T(8,128)(2,1)S(1)} %all_to_all.10.got_ref), custom_call_target="tpu_custom_call" | custom-call | tf_op jit(solution)/shard_map/pallas_call | solution.py:177
  18.5 10.3 %all_to_all.11 = bf16[16,8,512]{2,1,0:T(8,128)(2,1)S(1)} all-to-all(bf16[16,8,512]{2,1,0:T(8,128)(2,1)S(1)} %shard_map.29), channel_id=1, replica_groups={{13,5,12,4,15,7,14,6,9,1,8,0,11,3,10,2},{29,21,28,20,31,23,30,22,25,17,..., dimensions={0} | all-to-all | bytes 262144 | tf_op jit(solution)/shard_map/all_to_all | solution.py:122
  28.8 0.7 %copy.3 = bf16[2,8,16,256]{3,1,2,0:T(8,128)(2,1)} copy(bf16[2,8,16,256]{3,1,0,2:T(8,128)(2,1)S(1)} %bitcast.4) | data formatting | bytes 262144 | tf_op jit(solution)/shard_map/transpose | solution.py:187

commit v17 on v16

--- a/solution.py
+++ b/solution.py
@@ -130,7 +130,7 @@
     row = peers // quarter
     half = quarter // 2
     rows = list(range(half, quarter)) + list(range(half))
-    across = rows[::half] + rows[1::half] if quarter == 4 else rows
+    across = [half, half - 1, quarter - 1, 0] if quarter == 4 else rows
     first = [z * row + i for z in across for i in range(row - 1, -1, -1)]
     second = [z * row + i for z in rows for i in range(row - 1, -1, -1)]
     return first, second

time: 29.9 us -> 29.9 us (level)
  no operation moved by 1% of the time
where the time goes in v17:
time: 29.9 us; the launch traced here: 29.4 us
  blocking collectives  27.1 us (91%)
  Pallas kernels  1.68 us (6%)
  local copies, waits for them, and re-layouts  0.66 us (2%)
    all_to_all x2, blocking collectives, exchange(): lax.all_to_all(blocks, AXES, split_axis=0, concat_axis=0, axis_index_grou...  27.1 us
    pallas_call x1, Pallas kernels, shards(): pl.pallas_call(functools.partial(pack_kernel, steps, block_of, heads, ctx...  1.11 us
    transpose x1, local copies, waits for them, and re-layouts, shards(): back.reshape(groups, tok_rows, steps, heads * head_dim)  0.66 us

profile of v17, /device:TPU:0, one launch (start us, length us, event | category | flops | bytes accessed | tf_op | source)
XLA Modules:
  0.0 29.4 jit_solution(13011791029676249500)
XLA Ops:
  0.0 1.1 %shard_map.28 = bf16[16,8,1792]{2,1,0:T(8,128)(2,1)S(1)} custom-call(bf16[2,1,8,12288]{3,2,1,0:T(8,128)(2,1)} %qkv_hbm.1, bf16[4,8192]{1,0:T(4,128)(2,1)} %ctx_hbm.1), custom_call_target="tpu_custom_call" | custom-call | tf_op jit(solution)/shard_map/pallas_call | solution.py:161
  1.1 18.0 %all_to_all.10.got_ref = bf16[16,8,1792]{2,1,0:T(8,128)(2,1)S(1)} all-to-all(bf16[16,8,1792]{2,1,0:T(8,128)(2,1)S(1)} %shard_map.28), channel_id=1, replica_groups={{13,5,12,4,11,3,10,2,15,7,14,6,9,1,8,0},{29,21,28,20,27,19,26,18,31,23,..., dimensions={0} | all-to-all | bytes 917504 | tf_op jit(solution)/shard_map/all_to_all | solution.py:122
  19.1 0.6 %shard_map.29 = bf16[16,8,512]{2,1,0:T(8,128)(2,1)S(1)} custom-call(bf16[16,8,1792]{2,1,0:T(8,128)(2,1)S(1)} %all_to_all.10.got_ref), custom_call_target="tpu_custom_call" | custom-call | tf_op jit(solution)/shard_map/pallas_call | solution.py:177
  19.7 9.1 %all_to_all.11 = bf16[16,8,512]{2,1,0:T(8,128)(2,1)S(1)} all-to-all(bf16[16,8,512]{2,1,0:T(8,128)(2,1)S(1)} %shard_map.29), channel_id=1, replica_groups={{13,5,12,4,15,7,14,6,9,1,8,0,11,3,10,2},{29,21,28,20,31,23,30,22,25,17,..., dimensions={0} | all-to-all | bytes 262144 | tf_op jit(solution)/shard_map/all_to_all | solution.py:122
  28.8 0.7 %copy.3 = bf16[2,8,16,256]{3,1,2,0:T(8,128)(2,1)} copy(bf16[2,8,16,256]{3,1,0,2:T(8,128)(2,1)S(1)} %bitcast.4) | data formatting | bytes 262144 | tf_op jit(solution)/shard_map/transpose | solution.py:187

commit v18 on v11

--- a/solution.py
+++ b/solution.py
@@ -44,39 +44,71 @@
         rows = slice(head * ctx_rows, (head + 1) * ctx_rows)
         return got_ref[:, rows, base : base + head_dim].reshape(sources * ctx_rows, head_dim)
 
-    tasks = []
+    def with_ones(vals):
+        return jnp.concatenate([vals, jnp.ones_like(vals)], axis=1)
+
+    def product(left, right):
+        return lax.dot_general(
+            left, right, (((1,), (1,)), ((), ())), preferred_element_type=jnp.float32
+        )
+
+    last = sections - 1
+    ctx_tokens = sources * ctx_rows
+    tokens = len(came_from[0]) * tok_rows
+    blocks = [(step, s) for step in range(steps) for s in range(sections)]
+    shared = [s == last and step + 1 < steps for step, s in blocks]
+    allowed = [
+        ctx_tokens + (step + is_shared) * tokens
+        for (step, _), is_shared in zip(blocks, shared)
+    ]
+    every_task = []
     for head in range(heads):
-        earlier = [(context(head, 0), context(head, 1))]
-        for step in range(steps):
-            own = [(part(step, s, head, 1), part(step, s, head, 2)) for s in range(sections)]
-            for s in range(sections):
-                pairs = earlier + [own[s]]
-                keys = jnp.concatenate([k for k, _ in pairs], axis=0)
-                vals = jnp.concatenate([v for _, v in pairs], axis=0)
-                tasks.append((step, s, head, part(step, s, head, 0), keys, vals))
-            earlier = earlier + [own[sections - 1]]
-    all_scores = [
-        lax.dot_general(q, k, (((1,), (1,)), ((), ())), preferred_element_type=jnp.float32)
-        for _, _, _, q, k, _ in tasks
-    ]
-    all_tops = [jnp.max(scores, axis=1, keepdims=True) for scores in all_scores]
-    all_weights = [
-        jnp.exp2((scores - top) * log2_scale).astype(jnp.bfloat16)
-        for scores, top in zip(all_scores, all_tops)
-    ]
-    all_mixed = [
-        jnp.dot(
-            weights,
-            jnp.concatenate([vals, jnp.ones_like(vals)], axis=1),
+        earlier = [(step, last, head) for step in range(steps - 1)]
+        keys = jnp.concatenate([context(head, 0)] + [part(*e, 1) for e in earlier], axis=0)
+        vals = jnp.concatenate([context(head, 1)] + [part(*e, 2) for e in earlier], axis=0)
+        queries = [part(step, s, head, 0) for step, s in blocks]
+        scores = product(jnp.concatenate(queries, axis=0), keys)
+        lane = lax.broadcasted_iota(jnp.int32, (tokens, keys.shape[0]), 1)
+        tasks = []
+        for i, (step, s) in enumerate(blocks):
+            common = scores[i * tokens : (i + 1) * tokens]
+            if allowed[i] < keys.shape[0]:
+                common = jnp.where(lane < allowed[i], common, -jnp.inf)
+            own = None if shared[i] else product(queries[i], part(step, s, head, 1))
+            tasks.append((common, own))
+        every_task.append((tasks, vals))
+    every_weight = []
+    for tasks, _ in every_task:
+        weights = []
+        for common, own in tasks:
+            top = jnp.max(common, axis=1, keepdims=True)
+            if own is not None:
+                top = jnp.maximum(top, jnp.max(own, axis=1, keepdims=True))
+            weights.append(
+                [
+                    None if x is None else jnp.exp2((x - top) * log2_scale).astype(jnp.bfloat16)
+                    for x in (common, own)
+                ]
+            )
+        every_weight.append(weights)
+    for head, (weights, (_, vals)) in enumerate(zip(every_weight, every_task)):
+        mixed_all = jnp.dot(
+            jnp.concatenate([common for common, _ in weights], axis=0),
+            with_ones(vals),
             preferred_element_type=jnp.float32,
         )
-        for weights, (_, _, _, _, _, vals) in zip(all_weights, tasks)
-    ]
-    for mixed, (step, s, head, _, _, _) in zip(all_mixed, tasks):
-        done = (mixed[:, :head_dim] / mixed[:, head_dim:]).astype(jnp.bfloat16)
-        base = (step * heads + head) * head_dim
-        for slot, p in enumerate(goes_to[s]):
-            out_ref[p, :, base : base + head_dim] = done[slot * tok_rows : (slot + 1) * tok_rows]
+        for i, (step, s) in enumerate(blocks):
+            mixed = mixed_all[i * tokens : (i + 1) * tokens]
+            if not shared[i]:
+                mixed = mixed + jnp.dot(
+                    weights[i][1],
+                    with_ones(part(step, s, head, 2)),
+                    preferred_element_type=jnp.float32,
+                )
+            done = (mixed[:, :head_dim] / mixed[:, head_dim:]).astype(jnp.bfloat16)
+            base = (step * heads + head) * head_dim
+            for slot, p in enumerate(goes_to[s]):
+                out_ref[p, :, base : base + head_dim] = done[slot * tok_rows : (slot + 1) * tok_rows]
 
 
 def pack_kernel(
@@ -149,7 +181,7 @@
     if copies > 1 or heads * ctx_rows != tok_rows:
         return shards_copied(qkv_all, context_kv, sections, groups, copies, heads, scale)
 
-    chunks = math.gcd(groups, 2)
+    chunks = 1
     per_section = peers // sections
     first, second = send_orders(sections, per_section)
     devices = range(sections * per_section)

time: 29.1 us -> 29.1 us (level)
  no operation moved by 1% of the time
where the time goes in v18:
time: 29.1 us; the launch traced here: 28.7 us
  blocking collectives  26.4 us (91%)
  Pallas kernels  1.61 us (6%)
  local copies, waits for them, and re-layouts  0.66 us (2%)
    all_to_all x2, blocking collectives, exchange(): lax.all_to_all(blocks, AXES, split_axis=0, concat_axis=0, axis_index_grou...  26.4 us
    pallas_call x1, Pallas kernels, shards(): pl.pallas_call(functools.partial(pack_kernel, steps, block_of, heads, ctx...  1.09 us
    transpose x1, local copies, waits for them, and re-layouts, shards(): back.reshape(groups, tok_rows, steps, heads * head_dim)  0.66 us

profile of v18, /device:TPU:0, one launch (start us, length us, event | category | flops | bytes accessed | tf_op | source)
XLA Modules:
  0.0 28.7 jit_solution(16253311705571174126)
XLA Ops:
  0.0 1.1 %shard_map.28 = bf16[16,8,1792]{2,1,0:T(8,128)(2,1)S(1)} custom-call(bf16[2,1,8,12288]{3,2,1,0:T(8,128)(2,1)} %qkv_hbm.1, bf16[4,8192]{1,0:T(4,128)(2,1)} %ctx_hbm.1), custom_call_target="tpu_custom_call" | custom-call | tf_op jit(solution)/shard_map/pallas_call | solution.py:193
  1.1 18.0 %all_to_all.10.got_ref = bf16[16,8,1792]{2,1,0:T(8,128)(2,1)S(1)} all-to-all(bf16[16,8,1792]{2,1,0:T(8,128)(2,1)S(1)} %shard_map.28), channel_id=1, replica_groups={{13,5,12,4,11,3,10,2,9,1,8,0,15,7,14,6},{29,21,28,20,27,19,26,18,25,17,..., dimensions={0} | all-to-all | bytes 917504 | tf_op jit(solution)/shard_map/all_to_all | solution.py:154
  19.1 0.5 %shard_map.29 = bf16[16,8,512]{2,1,0:T(8,128)(2,1)S(1)} custom-call(bf16[16,8,1792]{2,1,0:T(8,128)(2,1)S(1)} %all_to_all.10.got_ref), custom_call_target="tpu_custom_call" | custom-call | tf_op jit(solution)/shard_map/pallas_call | solution.py:209
  19.6 8.4 %all_to_all.11 = bf16[16,8,512]{2,1,0:T(8,128)(2,1)S(1)} all-to-all(bf16[16,8,512]{2,1,0:T(8,128)(2,1)S(1)} %shard_map.29), channel_id=1, replica_groups={{13,5,12,4,15,7,14,6,9,1,8,0,11,3,10,2},{29,21,28,20,31,23,30,22,25,17,..., dimensions={0} | all-to-all | bytes 262144 | tf_op jit(solution)/shard_map/all_to_all | solution.py:154
  28.0 0.7 %copy.3 = bf16[2,8,16,256]{3,1,2,0:T(8,128)(2,1)} copy(bf16[2,8,16,256]{3,1,0,2:T(8,128)(2,1)S(1)} %bitcast.4) | data formatting | bytes 262144 | tf_op jit(solution)/shard_map/transpose | solution.py:219

commit v19 on v18

--- a/solution.py
+++ b/solution.py
@@ -160,11 +160,12 @@
     peers = sections * per_section
     quarter = math.gcd(peers, 4)
     row = peers // quarter
-    turned = [z * row + i for z in range(quarter - 1, -1, -1) for i in range(row - 1, -1, -1)]
+    inner = [i + s for i in range(row - sections, -1, -sections) for s in range(sections)]
+    turned = [z * row + i for z in range(quarter - 1, -1, -1) for i in inner]
     first = turned[row:] + turned[:row]
     half = quarter // 2
     rows = list(range(half, quarter)) + list(range(half))
-    second = [z * row + i for z in rows for i in range(row - 1, -1, -1)]
+    second = [z * row + i for z in rows for i in inner]
     return first, second
 
 

time: 29.1 us -> 30 us (1.031)
  blocking collectives: 26.4 us -> 27.4 us
    all_to_all x2, blocking collectives: 26.4 us -> 27.4 us  [exchange(): lax.all_to_all(blocks, AXES, split_axis=0, concat_axis=0, axis_index_grou...]
where the time goes in v19:
time: 30 us; the launch traced here: 29.6 us
  blocking collectives  27.4 us (91%)
  Pallas kernels  1.61 us (5%)
  local copies, waits for them, and re-layouts  0.66 us (2%)
    all_to_all x2, blocking collectives, exchange(): lax.all_to_all(blocks, AXES, split_axis=0, concat_axis=0, axis_index_grou...  27.4 us
    pallas_call x1, Pallas kernels, shards(): pl.pallas_call(functools.partial(pack_kernel, steps, block_of, heads, ctx...  1.09 us
    transpose x1, local copies, waits for them, and re-layouts, shards(): back.reshape(groups, tok_rows, steps, heads * head_dim)  0.66 us

profile of v19, /device:TPU:0, one launch (start us, length us, event | category | flops | bytes accessed | tf_op | source)
XLA Modules:
  0.0 29.6 jit_solution(11141676318440892297)
XLA Ops:
  0.0 1.1 %shard_map.28 = bf16[16,8,1792]{2,1,0:T(8,128)(2,1)S(1)} custom-call(bf16[2,1,8,12288]{3,2,1,0:T(8,128)(2,1)} %qkv_hbm.1, bf16[4,8192]{1,0:T(4,128)(2,1)} %ctx_hbm.1), custom_call_target="tpu_custom_call" | custom-call | tf_op jit(solution)/shard_map/pallas_call | solution.py:194
  1.1 18.8 %all_to_all.10.got_ref = bf16[16,8,1792]{2,1,0:T(8,128)(2,1)S(1)} all-to-all(bf16[16,8,1792]{2,1,0:T(8,128)(2,1)S(1)} %shard_map.28), channel_id=1, replica_groups={{5,13,4,12,3,11,2,10,1,9,0,8,7,15,6,14},{21,29,20,28,19,27,18,26,17,25,..., dimensions={0} | all-to-all | bytes 917504 | tf_op jit(solution)/shard_map/all_to_all | solution.py:154
  19.9 0.5 %shard_map.29 = bf16[16,8,512]{2,1,0:T(8,128)(2,1)S(1)} custom-call(bf16[16,8,1792]{2,1,0:T(8,128)(2,1)S(1)} %all_to_all.10.got_ref), custom_call_target="tpu_custom_call" | custom-call | tf_op jit(solution)/shard_map/pallas_call | solution.py:210
  20.4 8.5 %all_to_all.11 = bf16[16,8,512]{2,1,0:T(8,128)(2,1)S(1)} all-to-all(bf16[16,8,512]{2,1,0:T(8,128)(2,1)S(1)} %shard_map.29), channel_id=1, replica_groups={{5,13,4,12,7,15,6,14,1,9,0,8,3,11,2,10},{21,29,20,28,23,31,22,30,17,25,..., dimensions={0} | all-to-all | bytes 262144 | tf_op jit(solution)/shard_map/all_to_all | solution.py:154
  29.0 0.7 %copy.3 = bf16[2,8,16,256]{3,1,2,0:T(8,128)(2,1)} copy(bf16[2,8,16,256]{3,1,0,2:T(8,128)(2,1)S(1)} %bitcast.4) | data formatting | bytes 262144 | tf_op jit(solution)/shard_map/transpose | solution.py:220

commit v20 on v19

--- a/solution.py
+++ b/solution.py
@@ -160,7 +160,7 @@
     peers = sections * per_section
     quarter = math.gcd(peers, 4)
     row = peers // quarter
-    inner = [i + s for i in range(row - sections, -1, -sections) for s in range(sections)]
+    inner = [i + s for i in range(0, row, sections) for s in range(sections - 1, -1, -1)]
     turned = [z * row + i for z in range(quarter - 1, -1, -1) for i in inner]
     first = turned[row:] + turned[:row]
     half = quarter // 2

time: 30 us -> 31 us (1.033)
  blocking collectives: 27.4 us -> 28.5 us
    all_to_all x2, blocking collectives: 27.4 us -> 28.5 us  [exchange(): lax.all_to_all(blocks, AXES, split_axis=0, concat_axis=0, axis_index_grou...]
where the time goes in v20:
time: 31 us; the launch traced here: 30.7 us
  blocking collectives  28.5 us (92%)
  Pallas kernels  1.61 us (5%)
  local copies, waits for them, and re-layouts  0.66 us (2%)
    all_to_all x2, blocking collectives, exchange(): lax.all_to_all(blocks, AXES, split_axis=0, concat_axis=0, axis_index_grou...  28.5 us
    pallas_call x1, Pallas kernels, shards(): pl.pallas_call(functools.partial(pack_kernel, steps, block_of, heads, ctx...  1.09 us
    transpose x1, local copies, waits for them, and re-layouts, shards(): back.reshape(groups, tok_rows, steps, heads * head_dim)  0.66 us

profile of v20, /device:TPU:0, one launch (start us, length us, event | category | flops | bytes accessed | tf_op | source)
XLA Modules:
  0.0 30.7 jit_solution(10664683343199866510)
XLA Ops:
  0.0 1.1 %shard_map.28 = bf16[16,8,1792]{2,1,0:T(8,128)(2,1)S(1)} custom-call(bf16[2,1,8,12288]{3,2,1,0:T(8,128)(2,1)} %qkv_hbm.1, bf16[4,8192]{1,0:T(4,128)(2,1)} %ctx_hbm.1), custom_call_target="tpu_custom_call" | custom-call | tf_op jit(solution)/shard_map/pallas_call | solution.py:194
  1.1 18.0 %all_to_all.10.got_ref = bf16[16,8,1792]{2,1,0:T(8,128)(2,1)S(1)} all-to-all(bf16[16,8,1792]{2,1,0:T(8,128)(2,1)S(1)} %shard_map.28), channel_id=1, replica_groups={{12,4,13,5,10,2,11,3,8,0,9,1,14,6,15,7},{28,20,29,21,26,18,27,19,24,16,..., dimensions={0} | all-to-all | bytes 917504 | tf_op jit(solution)/shard_map/all_to_all | solution.py:154
  19.1 0.5 %shard_map.29 = bf16[16,8,512]{2,1,0:T(8,128)(2,1)S(1)} custom-call(bf16[16,8,1792]{2,1,0:T(8,128)(2,1)S(1)} %all_to_all.10.got_ref), custom_call_target="tpu_custom_call" | custom-call | tf_op jit(solution)/shard_map/pallas_call | solution.py:210
  19.6 10.4 %all_to_all.11 = bf16[16,8,512]{2,1,0:T(8,128)(2,1)S(1)} all-to-all(bf16[16,8,512]{2,1,0:T(8,128)(2,1)S(1)} %shard_map.29), channel_id=1, replica_groups={{12,4,13,5,14,6,15,7,8,0,9,1,10,2,11,3},{28,20,29,21,30,22,31,23,24,16,..., dimensions={0} | all-to-all | bytes 262144 | tf_op jit(solution)/shard_map/all_to_all | solution.py:154
  30.1 0.7 %copy.3 = bf16[2,8,16,256]{3,1,2,0:T(8,128)(2,1)} copy(bf16[2,8,16,256]{3,1,0,2:T(8,128)(2,1)S(1)} %bitcast.4) | data formatting | bytes 262144 | tf_op jit(solution)/shard_map/transpose | solution.py:220

commit v21 on v18

--- a/solution.py
+++ b/solution.py
@@ -160,9 +160,9 @@
     peers = sections * per_section
     quarter = math.gcd(peers, 4)
     row = peers // quarter
-    turned = [z * row + i for z in range(quarter - 1, -1, -1) for i in range(row - 1, -1, -1)]
-    first = turned[row:] + turned[:row]
     half = quarter // 2
+    halves = list(range(half, quarter)) + list(range(half - 1, -1, -1))
+    first = [z * row + i for z in halves for i in range(row - 1, -1, -1)]
     rows = list(range(half, quarter)) + list(range(half))
     second = [z * row + i for z in rows for i in range(row - 1, -1, -1)]
     return first, second

time: 29.1 us -> 29.3 us (level)
  no operation moved by 1% of the time
where the time goes in v21:
time: 29.3 us; the launch traced here: 28.8 us
  blocking collectives  26.5 us (90%)
  Pallas kernels  1.61 us (5%)
  local copies, waits for them, and re-layouts  0.66 us (2%)
    all_to_all x2, blocking collectives, exchange(): lax.all_to_all(blocks, AXES, split_axis=0, concat_axis=0, axis_index_grou...  26.5 us
    pallas_call x1, Pallas kernels, shards(): pl.pallas_call(functools.partial(pack_kernel, steps, block_of, heads, ctx...  1.09 us
    transpose x1, local copies, waits for them, and re-layouts, shards(): back.reshape(groups, tok_rows, steps, heads * head_dim)  0.66 us

profile of v21, /device:TPU:0, one launch (start us, length us, event | category | flops | bytes accessed | tf_op | source)
XLA Modules:
  0.0 28.8 jit_solution(6985319090299228134)
XLA Ops:
  0.0 1.1 %shard_map.28 = bf16[16,8,1792]{2,1,0:T(8,128)(2,1)S(1)} custom-call(bf16[2,1,8,12288]{3,2,1,0:T(8,128)(2,1)} %qkv_hbm.1, bf16[4,8192]{1,0:T(4,128)(2,1)} %ctx_hbm.1), custom_call_target="tpu_custom_call" | custom-call | tf_op jit(solution)/shard_map/pallas_call | solution.py:193
  1.1 18.3 %all_to_all.10.got_ref = bf16[16,8,1792]{2,1,0:T(8,128)(2,1)S(1)} all-to-all(bf16[16,8,1792]{2,1,0:T(8,128)(2,1)S(1)} %shard_map.28), channel_id=1, replica_groups={{13,5,12,4,15,7,14,6,11,3,10,2,9,1,8,0},{29,21,28,20,31,23,30,22,27,19,..., dimensions={0} | all-to-all | bytes 917504 | tf_op jit(solution)/shard_map/all_to_all | solution.py:154
  19.4 0.5 %shard_map.29 = bf16[16,8,512]{2,1,0:T(8,128)(2,1)S(1)} custom-call(bf16[16,8,1792]{2,1,0:T(8,128)(2,1)S(1)} %all_to_all.10.got_ref), custom_call_target="tpu_custom_call" | custom-call | tf_op jit(solution)/shard_map/pallas_call | solution.py:209
  20.0 8.2 %all_to_all.11 = bf16[16,8,512]{2,1,0:T(8,128)(2,1)S(1)} all-to-all(bf16[16,8,512]{2,1,0:T(8,128)(2,1)S(1)} %shard_map.29), channel_id=1, replica_groups={{13,5,12,4,15,7,14,6,9,1,8,0,11,3,10,2},{29,21,28,20,31,23,30,22,25,17,..., dimensions={0} | all-to-all | bytes 262144 | tf_op jit(solution)/shard_map/all_to_all | solution.py:154
  28.1 0.7 %copy.3 = bf16[2,8,16,256]{3,1,2,0:T(8,128)(2,1)} copy(bf16[2,8,16,256]{3,1,0,2:T(8,128)(2,1)S(1)} %bitcast.4) | data formatting | bytes 262144 | tf_op jit(solution)/shard_map/transpose | solution.py:219

commit v22 on v18

--- a/solution.py
+++ b/solution.py
@@ -163,7 +163,7 @@
     turned = [z * row + i for z in range(quarter - 1, -1, -1) for i in range(row - 1, -1, -1)]
     first = turned[row:] + turned[:row]
     half = quarter // 2
-    rows = list(range(half, quarter)) + list(range(half))
+    rows = list(range(half - 1, quarter)) + list(range(half - 1))
     second = [z * row + i for z in rows for i in range(row - 1, -1, -1)]
     return first, second
 

time: 29.1 us -> 29.4 us (1.010)
  blocking collectives: 26.4 us -> 26.7 us
    all_to_all x2, blocking collectives: 26.4 us -> 26.7 us  [exchange(): lax.all_to_all(blocks, AXES, split_axis=0, concat_axis=0, axis_index_grou...]
where the time goes in v22:
time: 29.4 us; the launch traced here: 29 us
  blocking collectives  26.7 us (91%)
  Pallas kernels  1.61 us (5%)
  local copies, waits for them, and re-layouts  0.66 us (2%)
    all_to_all x2, blocking collectives, exchange(): lax.all_to_all(blocks, AXES, split_axis=0, concat_axis=0, axis_index_grou...  26.7 us
    pallas_call x1, Pallas kernels, shards(): pl.pallas_call(functools.partial(pack_kernel, steps, block_of, heads, ctx...  1.09 us
    transpose x1, local copies, waits for them, and re-layouts, shards(): back.reshape(groups, tok_rows, steps, heads * head_dim)  0.66 us

profile of v22, /device:TPU:0, one launch (start us, length us, event | category | flops | bytes accessed | tf_op | source)
XLA Modules:
  0.0 29.0 jit_solution(12094622102080976863)
XLA Ops:
  0.0 1.1 %shard_map.28 = bf16[16,8,1792]{2,1,0:T(8,128)(2,1)S(1)} custom-call(bf16[2,1,8,12288]{3,2,1,0:T(8,128)(2,1)} %qkv_hbm.1, bf16[4,8192]{1,0:T(4,128)(2,1)} %ctx_hbm.1), custom_call_target="tpu_custom_call" | custom-call | tf_op jit(solution)/shard_map/pallas_call | solution.py:193
  1.1 18.0 %all_to_all.10.got_ref = bf16[16,8,1792]{2,1,0:T(8,128)(2,1)S(1)} all-to-all(bf16[16,8,1792]{2,1,0:T(8,128)(2,1)S(1)} %shard_map.28), channel_id=1, replica_groups={{13,5,12,4,11,3,10,2,9,1,8,0,15,7,14,6},{29,21,28,20,27,19,26,18,25,17,..., dimensions={0} | all-to-all | bytes 917504 | tf_op jit(solution)/shard_map/all_to_all | solution.py:154
  19.1 0.5 %shard_map.29 = bf16[16,8,512]{2,1,0:T(8,128)(2,1)S(1)} custom-call(bf16[16,8,1792]{2,1,0:T(8,128)(2,1)S(1)} %all_to_all.10.got_ref), custom_call_target="tpu_custom_call" | custom-call | tf_op jit(solution)/shard_map/pallas_call | solution.py:209
  19.6 8.7 %all_to_all.11 = bf16[16,8,512]{2,1,0:T(8,128)(2,1)S(1)} all-to-all(bf16[16,8,512]{2,1,0:T(8,128)(2,1)S(1)} %shard_map.29), channel_id=1, replica_groups={{11,3,10,2,13,5,12,4,15,7,14,6,9,1,8,0},{27,19,26,18,29,21,28,20,31,23,..., dimensions={0} | all-to-all | bytes 262144 | tf_op jit(solution)/shard_map/all_to_all | solution.py:154
  28.3 0.7 %copy.3 = bf16[2,8,16,256]{3,1,2,0:T(8,128)(2,1)} copy(bf16[2,8,16,256]{3,1,0,2:T(8,128)(2,1)S(1)} %bitcast.4) | data formatting | bytes 262144 | tf_op jit(solution)/shard_map/transpose | solution.py:219

commit v23 on v22

--- a/solution.py
+++ b/solution.py
@@ -163,7 +163,7 @@
     turned = [z * row + i for z in range(quarter - 1, -1, -1) for i in range(row - 1, -1, -1)]
     first = turned[row:] + turned[:row]
     half = quarter // 2
-    rows = list(range(half - 1, quarter)) + list(range(half - 1))
+    rows = [half] + list(range(half)) + list(range(half + 1, quarter))
     second = [z * row + i for z in rows for i in range(row - 1, -1, -1)]
     return first, second
 

time: 29.4 us -> 29.3 us (level)
  no operation moved by 1% of the time
where the time goes in v23:
time: 29.3 us; the launch traced here: 29 us
  blocking collectives  26.7 us (91%)
  Pallas kernels  1.61 us (5%)
  local copies, waits for them, and re-layouts  0.66 us (2%)
    all_to_all x2, blocking collectives, exchange(): lax.all_to_all(blocks, AXES, split_axis=0, concat_axis=0, axis_index_grou...  26.7 us
    pallas_call x1, Pallas kernels, shards(): pl.pallas_call(functools.partial(pack_kernel, steps, block_of, heads, ctx...  1.09 us
    transpose x1, local copies, waits for them, and re-layouts, shards(): back.reshape(groups, tok_rows, steps, heads * head_dim)  0.66 us

profile of v23, /device:TPU:0, one launch (start us, length us, event | category | flops | bytes accessed | tf_op | source)
XLA Modules:
  0.0 29.0 jit_solution(13698197461017977272)
XLA Ops:
  0.0 1.1 %shard_map.28 = bf16[16,8,1792]{2,1,0:T(8,128)(2,1)S(1)} custom-call(bf16[2,1,8,12288]{3,2,1,0:T(8,128)(2,1)} %qkv_hbm.1, bf16[4,8192]{1,0:T(4,128)(2,1)} %ctx_hbm.1), custom_call_target="tpu_custom_call" | custom-call | tf_op jit(solution)/shard_map/pallas_call | solution.py:193
  1.1 18.0 %all_to_all.10.got_ref = bf16[16,8,1792]{2,1,0:T(8,128)(2,1)S(1)} all-to-all(bf16[16,8,1792]{2,1,0:T(8,128)(2,1)S(1)} %shard_map.28), channel_id=1, replica_groups={{13,5,12,4,11,3,10,2,9,1,8,0,15,7,14,6},{29,21,28,20,27,19,26,18,25,17,..., dimensions={0} | all-to-all | bytes 917504 | tf_op jit(solution)/shard_map/all_to_all | solution.py:154
  19.1 0.5 %shard_map.29 = bf16[16,8,512]{2,1,0:T(8,128)(2,1)S(1)} custom-call(bf16[16,8,1792]{2,1,0:T(8,128)(2,1)S(1)} %all_to_all.10.got_ref), custom_call_target="tpu_custom_call" | custom-call | tf_op jit(solution)/shard_map/pallas_call | solution.py:209
  19.6 8.8 %all_to_all.11 = bf16[16,8,512]{2,1,0:T(8,128)(2,1)S(1)} all-to-all(bf16[16,8,512]{2,1,0:T(8,128)(2,1)S(1)} %shard_map.29), channel_id=1, replica_groups={{13,5,12,4,9,1,8,0,11,3,10,2,15,7,14,6},{29,21,28,20,25,17,24,16,27,19,..., dimensions={0} | all-to-all | bytes 262144 | tf_op jit(solution)/shard_map/all_to_all | solution.py:154
  28.4 0.7 %copy.3 = bf16[2,8,16,256]{3,1,2,0:T(8,128)(2,1)} copy(bf16[2,8,16,256]{3,1,0,2:T(8,128)(2,1)S(1)} %bitcast.4) | data formatting | bytes 262144 | tf_op jit(solution)/shard_map/transpose | solution.py:219

commit v24 on v23

--- a/solution.py
+++ b/solution.py
@@ -163,7 +163,8 @@
     turned = [z * row + i for z in range(quarter - 1, -1, -1) for i in range(row - 1, -1, -1)]
     first = turned[row:] + turned[:row]
     half = quarter // 2
-    rows = [half] + list(range(half)) + list(range(half + 1, quarter))
+    rows = sorted(range(quarter), key=lambda z: (abs(z - half) > 1, abs(z - half), z))
+    rows = [z for z in rows if z <= half and z] + [z for z in rows if z > half] + [0]
     second = [z * row + i for z in rows for i in range(row - 1, -1, -1)]
     return first, second
 

time: 29.3 us -> 29.1 us (level)
  blocking collectives: 26.7 us -> 26.4 us
    all_to_all x2, blocking collectives: 26.7 us -> 26.4 us  [exchange(): lax.all_to_all(blocks, AXES, split_axis=0, concat_axis=0, axis_index_grou...]
where the time goes in v24:
time: 29.1 us; the launch traced here: 28.7 us
  blocking collectives  26.4 us (91%)
  Pallas kernels  1.61 us (6%)
  local copies, waits for them, and re-layouts  0.66 us (2%)
    all_to_all x2, blocking collectives, exchange(): lax.all_to_all(blocks, AXES, split_axis=0, concat_axis=0, axis_index_grou...  26.4 us
    pallas_call x1, Pallas kernels, shards(): pl.pallas_call(functools.partial(pack_kernel, steps, block_of, heads, ctx...  1.09 us
    transpose x1, local copies, waits for them, and re-layouts, shards(): back.reshape(groups, tok_rows, steps, heads * head_dim)  0.66 us

profile of v24, /device:TPU:0, one launch (start us, length us, event | category | flops | bytes accessed | tf_op | source)
XLA Modules:
  0.0 28.7 jit_solution(5904974555322072016)
XLA Ops:
  0.0 1.1 %shard_map.28 = bf16[16,8,1792]{2,1,0:T(8,128)(2,1)S(1)} custom-call(bf16[2,1,8,12288]{3,2,1,0:T(8,128)(2,1)} %qkv_hbm.1, bf16[4,8192]{1,0:T(4,128)(2,1)} %ctx_hbm.1), custom_call_target="tpu_custom_call" | custom-call | tf_op jit(solution)/shard_map/pallas_call | solution.py:194
  1.1 18.0 %all_to_all.10.got_ref = bf16[16,8,1792]{2,1,0:T(8,128)(2,1)S(1)} all-to-all(bf16[16,8,1792]{2,1,0:T(8,128)(2,1)S(1)} %shard_map.28), channel_id=1, replica_groups={{13,5,12,4,11,3,10,2,9,1,8,0,15,7,14,6},{29,21,28,20,27,19,26,18,25,17,..., dimensions={0} | all-to-all | bytes 917504 | tf_op jit(solution)/shard_map/all_to_all | solution.py:154
  19.1 0.5 %shard_map.29 = bf16[16,8,512]{2,1,0:T(8,128)(2,1)S(1)} custom-call(bf16[16,8,1792]{2,1,0:T(8,128)(2,1)S(1)} %all_to_all.10.got_ref), custom_call_target="tpu_custom_call" | custom-call | tf_op jit(solution)/shard_map/pallas_call | solution.py:210
  19.6 8.4 %all_to_all.11 = bf16[16,8,512]{2,1,0:T(8,128)(2,1)S(1)} all-to-all(bf16[16,8,512]{2,1,0:T(8,128)(2,1)S(1)} %shard_map.29), channel_id=1, replica_groups={{13,5,12,4,11,3,10,2,15,7,14,6,9,1,8,0},{29,21,28,20,27,19,26,18,31,23,..., dimensions={0} | all-to-all | bytes 262144 | tf_op jit(solution)/shard_map/all_to_all | solution.py:154
  28.0 0.7 %copy.3 = bf16[2,8,16,256]{3,1,2,0:T(8,128)(2,1)} copy(bf16[2,8,16,256]{3,1,0,2:T(8,128)(2,1)S(1)} %bitcast.4) | data formatting | bytes 262144 | tf_op jit(solution)/shard_map/transpose | solution.py:220

commit v25 on v21

--- a/solution.py
+++ b/solution.py
@@ -161,8 +161,8 @@
     quarter = math.gcd(peers, 4)
     row = peers // quarter
     half = quarter // 2
-    halves = list(range(half, quarter)) + list(range(half - 1, -1, -1))
-    first = [z * row + i for z in halves for i in range(row - 1, -1, -1)]
+    spread = [half] + list(range(half)) + list(range(half + 1, quarter))
+    first = [z * row + i for z in spread for i in range(row - 1, -1, -1)]
     rows = list(range(half, quarter)) + list(range(half))
     second = [z * row + i for z in rows for i in range(row - 1, -1, -1)]
     return first, second

time: 29.3 us -> 29.8 us (1.017)
  blocking collectives: 26.5 us -> 27.1 us
    all_to_all x2, blocking collectives: 26.5 us -> 27.1 us  [exchange(): lax.all_to_all(blocks, AXES, split_axis=0, concat_axis=0, axis_index_grou...]
where the time goes in v25:
time: 29.8 us; the launch traced here: 29.4 us
  blocking collectives  27.1 us (91%)
  Pallas kernels  1.61 us (5%)
  local copies, waits for them, and re-layouts  0.66 us (2%)
    all_to_all x2, blocking collectives, exchange(): lax.all_to_all(blocks, AXES, split_axis=0, concat_axis=0, axis_index_grou...  27.1 us
    pallas_call x1, Pallas kernels, shards(): pl.pallas_call(functools.partial(pack_kernel, steps, block_of, heads, ctx...  1.09 us
    transpose x1, local copies, waits for them, and re-layouts, shards(): back.reshape(groups, tok_rows, steps, heads * head_dim)  0.66 us

profile of v25, /device:TPU:0, one launch (start us, length us, event | category | flops | bytes accessed | tf_op | source)
XLA Modules:
  0.0 29.4 jit_solution(1715211304034207534)
XLA Ops:
  0.0 1.1 %shard_map.28 = bf16[16,8,1792]{2,1,0:T(8,128)(2,1)S(1)} custom-call(bf16[2,1,8,12288]{3,2,1,0:T(8,128)(2,1)} %qkv_hbm.1, bf16[4,8192]{1,0:T(4,128)(2,1)} %ctx_hbm.1), custom_call_target="tpu_custom_call" | custom-call | tf_op jit(solution)/shard_map/pallas_call | solution.py:193
  1.1 15.6 %all_to_all.10.got_ref = bf16[16,8,1792]{2,1,0:T(8,128)(2,1)S(1)} all-to-all(bf16[16,8,1792]{2,1,0:T(8,128)(2,1)S(1)} %shard_map.28), channel_id=1, replica_groups={{13,5,12,4,9,1,8,0,11,3,10,2,15,7,14,6},{29,21,28,20,25,17,24,16,27,19,..., dimensions={0} | all-to-all | bytes 917504 | tf_op jit(solution)/shard_map/all_to_all | solution.py:154
  16.7 0.5 %shard_map.29 = bf16[16,8,512]{2,1,0:T(8,128)(2,1)S(1)} custom-call(bf16[16,8,1792]{2,1,0:T(8,128)(2,1)S(1)} %all_to_all.10.got_ref), custom_call_target="tpu_custom_call" | custom-call | tf_op jit(solution)/shard_map/pallas_call | solution.py:209
  17.2 11.5 %all_to_all.11 = bf16[16,8,512]{2,1,0:T(8,128)(2,1)S(1)} all-to-all(bf16[16,8,512]{2,1,0:T(8,128)(2,1)S(1)} %shard_map.29), channel_id=1, replica_groups={{13,5,12,4,15,7,14,6,9,1,8,0,11,3,10,2},{29,21,28,20,31,23,30,22,25,17,..., dimensions={0} | all-to-all | bytes 262144 | tf_op jit(solution)/shard_map/all_to_all | solution.py:154
  28.7 0.7 %copy.3 = bf16[2,8,16,256]{3,1,2,0:T(8,128)(2,1)} copy(bf16[2,8,16,256]{3,1,0,2:T(8,128)(2,1)S(1)} %bitcast.4) | data formatting | bytes 262144 | tf_op jit(solution)/shard_map/transpose | solution.py:219

commit v26 on v24

--- a/solution.py
+++ b/solution.py
@@ -105,7 +105,7 @@
                     with_ones(part(step, s, head, 2)),
                     preferred_element_type=jnp.float32,
                 )
-            done = (mixed[:, :head_dim] / mixed[:, head_dim:]).astype(jnp.bfloat16)
+            done = (mixed[:, :head_dim] * (1.0 / mixed[:, head_dim:])).astype(jnp.bfloat16)
             base = (step * heads + head) * head_dim
             for slot, p in enumerate(goes_to[s]):
                 out_ref[p, :, base : base + head_dim] = done[slot * tok_rows : (slot + 1) * tok_rows]
@@ -129,9 +129,9 @@
                     sems.at[step, chunk],
                 )
             )
-    ctx_copy.start()
     for copy in copies:
         copy.start()
+    ctx_copy.start()
     base = steps * width
     ctx_copy.wait()
     for group in range(groups):

time: 29.1 us -> 29.1 us (level)
  no operation moved by 1% of the time
where the time goes in v26:
time: 29.1 us; the launch traced here: 28.7 us
  blocking collectives  26.4 us (91%)
  Pallas kernels  1.62 us (6%)
  local copies, waits for them, and re-layouts  0.66 us (2%)
    all_to_all x2, blocking collectives, exchange(): lax.all_to_all(blocks, AXES, split_axis=0, concat_axis=0, axis_index_grou...  26.4 us
    pallas_call x1, Pallas kernels, shards(): pl.pallas_call(functools.partial(pack_kernel, steps, block_of, heads, ctx...  1.1 us
    transpose x1, local copies, waits for them, and re-layouts, shards(): back.reshape(groups, tok_rows, steps, heads * head_dim)  0.66 us

profile of v26, /device:TPU:0, one launch (start us, length us, event | category | flops | bytes accessed | tf_op | source)
XLA Modules:
  0.0 28.7 jit_solution(11731843677286079029)
XLA Ops:
  0.0 1.1 %shard_map.28 = bf16[16,8,1792]{2,1,0:T(8,128)(2,1)S(1)} custom-call(bf16[2,1,8,12288]{3,2,1,0:T(8,128)(2,1)} %qkv_hbm.1, bf16[4,8192]{1,0:T(4,128)(2,1)} %ctx_hbm.1), custom_call_target="tpu_custom_call" | custom-call | tf_op jit(solution)/shard_map/pallas_call | solution.py:194
  1.1 18.0 %all_to_all.10.got_ref = bf16[16,8,1792]{2,1,0:T(8,128)(2,1)S(1)} all-to-all(bf16[16,8,1792]{2,1,0:T(8,128)(2,1)S(1)} %shard_map.28), channel_id=1, replica_groups={{13,5,12,4,11,3,10,2,9,1,8,0,15,7,14,6},{29,21,28,20,27,19,26,18,25,17,..., dimensions={0} | all-to-all | bytes 917504 | tf_op jit(solution)/shard_map/all_to_all | solution.py:154
  19.1 0.5 %shard_map.29 = bf16[16,8,512]{2,1,0:T(8,128)(2,1)S(1)} custom-call(bf16[16,8,1792]{2,1,0:T(8,128)(2,1)S(1)} %all_to_all.10.got_ref), custom_call_target="tpu_custom_call" | custom-call | tf_op jit(solution)/shard_map/pallas_call | solution.py:210
  19.6 8.4 %all_to_all.11 = bf16[16,8,512]{2,1,0:T(8,128)(2,1)S(1)} all-to-all(bf16[16,8,512]{2,1,0:T(8,128)(2,1)S(1)} %shard_map.29), channel_id=1, replica_groups={{13,5,12,4,11,3,10,2,15,7,14,6,9,1,8,0},{29,21,28,20,27,19,26,18,31,23,..., dimensions={0} | all-to-all | bytes 262144 | tf_op jit(solution)/shard_map/all_to_all | solution.py:154
  28.0 0.7 %copy.3 = bf16[2,8,16,256]{3,1,2,0:T(8,128)(2,1)} copy(bf16[2,8,16,256]{3,1,0,2:T(8,128)(2,1)S(1)} %bitcast.4) | data formatting | bytes 262144 | tf_op jit(solution)/shard_map/transpose | solution.py:220

commit v27 on v26

--- a/solution.py
+++ b/solution.py
@@ -163,8 +163,7 @@
     turned = [z * row + i for z in range(quarter - 1, -1, -1) for i in range(row - 1, -1, -1)]
     first = turned[row:] + turned[:row]
     half = quarter // 2
-    rows = sorted(range(quarter), key=lambda z: (abs(z - half) > 1, abs(z - half), z))
-    rows = [z for z in rows if z <= half and z] + [z for z in rows if z > half] + [0]
+    rows = list(range(half, quarter)) + list(range(half))
     second = [z * row + i for z in rows for i in range(row - 1, -1, -1)]
     return first, second
 

time: 29.1 us -> 29.1 us (level)
  no operation moved by 1% of the time
where the time goes in v27:
time: 29.1 us; the launch traced here: 28.7 us
  blocking collectives  26.4 us (91%)
  Pallas kernels  1.62 us (6%)
  local copies, waits for them, and re-layouts  0.66 us (2%)
    all_to_all x2, blocking collectives, exchange(): lax.all_to_all(blocks, AXES, split_axis=0, concat_axis=0, axis_index_grou...  26.4 us
    pallas_call x1, Pallas kernels, shards(): pl.pallas_call(functools.partial(pack_kernel, steps, block_of, heads, ctx...  1.1 us
    transpose x1, local copies, waits for them, and re-layouts, shards(): back.reshape(groups, tok_rows, steps, heads * head_dim)  0.66 us

profile of v27, /device:TPU:0, one launch (start us, length us, event | category | flops | bytes accessed | tf_op | source)
XLA Modules:
  0.0 28.7 jit_solution(4125054347252561104)
XLA Ops:
  0.0 1.1 %shard_map.28 = bf16[16,8,1792]{2,1,0:T(8,128)(2,1)S(1)} custom-call(bf16[2,1,8,12288]{3,2,1,0:T(8,128)(2,1)} %qkv_hbm.1, bf16[4,8192]{1,0:T(4,128)(2,1)} %ctx_hbm.1), custom_call_target="tpu_custom_call" | custom-call | tf_op jit(solution)/shard_map/pallas_call | solution.py:193
  1.1 18.0 %all_to_all.10.got_ref = bf16[16,8,1792]{2,1,0:T(8,128)(2,1)S(1)} all-to-all(bf16[16,8,1792]{2,1,0:T(8,128)(2,1)S(1)} %shard_map.28), channel_id=1, replica_groups={{13,5,12,4,11,3,10,2,9,1,8,0,15,7,14,6},{29,21,28,20,27,19,26,18,25,17,..., dimensions={0} | all-to-all | bytes 917504 | tf_op jit(solution)/shard_map/all_to_all | solution.py:154
  19.1 0.5 %shard_map.29 = bf16[16,8,512]{2,1,0:T(8,128)(2,1)S(1)} custom-call(bf16[16,8,1792]{2,1,0:T(8,128)(2,1)S(1)} %all_to_all.10.got_ref), custom_call_target="tpu_custom_call" | custom-call | tf_op jit(solution)/shard_map/pallas_call | solution.py:209
  19.6 8.4 %all_to_all.11 = bf16[16,8,512]{2,1,0:T(8,128)(2,1)S(1)} all-to-all(bf16[16,8,512]{2,1,0:T(8,128)(2,1)S(1)} %shard_map.29), channel_id=1, replica_groups={{13,5,12,4,15,7,14,6,9,1,8,0,11,3,10,2},{29,21,28,20,31,23,30,22,25,17,..., dimensions={0} | all-to-all | bytes 262144 | tf_op jit(solution)/shard_map/all_to_all | solution.py:154
  28.0 0.7 %copy.3 = bf16[2,8,16,256]{3,1,2,0:T(8,128)(2,1)} copy(bf16[2,8,16,256]{3,1,0,2:T(8,128)(2,1)S(1)} %bitcast.4) | data formatting | bytes 262144 | tf_op jit(solution)/shard_map/transpose | solution.py:219
